TPU v7x, 32 devices: a whole 2x2x4 slice. The times are simulated.
32 devices in a mesh: ctx: 8 (over z, x), wsh: 4 (over y, core).
Axes of the slice: x: 2, y: 2, z: 4, core: 2. Of those that a mesh axis runs over, the one named last changes fastest.
Arguments:
- tokens: bfloat16 [4, 2048, 1024], P('wsh', 'ctx'), may hold values from -6 to 6
- block_map: int32 [8, 2], replicated, may hold values from 0 to 15, as said below
- positions: int32 [4, 2048], P('wsh'), may hold values from 0 to 255, as said below
- norm_gain_one: bfloat16 [1024], P('wsh'), may hold values from 0.5 to 1.5
- norm_shift_one: bfloat16 [1024], P('wsh'), may hold values from -2.5 to 2.5
- qkv_weight: bfloat16 [1024, 3072], P('wsh'), may hold values from -0.1875 to 0.1875
- query_bias: bfloat16 [1024], P('wsh'), may hold values from -2.5 to 2.5
- value_bias: bfloat16 [1024], P('wsh'), may hold values from -2.5 to 2.5
- dense_weight: bfloat16 [1024, 1024], P('wsh'), may hold values from -0.5 to 0.5
- dense_bias: bfloat16 [1024], P('wsh'), may hold values from -2.5 to 2.5
- norm_gain_two: bfloat16 [1024], P('wsh'), may hold values from 0.5 to 1.5
- norm_shift_two: bfloat16 [1024], P('wsh'), may hold values from -2.5 to 2.5
- up_weight: bfloat16 [1024, 4096], P('wsh'), may hold values from -0.1875 to 0.1875
- up_bias: bfloat16 [4096], P('wsh'), may hold values from -2.5 to 2.5
- down_weight: bfloat16 [4096, 1024], P('wsh'), may hold values from -0.09375 to 0.09375
- down_bias: bfloat16 [1024], P('wsh'), may hold values from -2.5 to 2.5
- cotangent: bfloat16 [4, 2048, 1024], P('wsh', 'ctx'), may hold values from -6 to 6
Outputs:
- layer_out: bfloat16 [4, 2048, 1024], P('wsh', 'ctx')
- input_grad: bfloat16 [4, 2048, 1024], P('wsh', 'ctx')
- grad_norm_gain_one: float32 [1024], P('wsh')
- grad_norm_shift_one: float32 [1024], P('wsh')
- grad_qkv_weight: float32 [1024, 3072], P('wsh')
- grad_query_bias: float32 [1024], P('wsh')
- grad_value_bias: float32 [1024], P('wsh')
- grad_dense_weight: float32 [1024, 1024], P('wsh')
- grad_dense_bias: float32 [1024], P('wsh')
- grad_norm_gain_two: float32 [1024], P('wsh')
- grad_norm_shift_two: float32 [1024], P('wsh')
- grad_up_weight: float32 [1024, 4096], P('wsh')
- grad_up_bias: float32 [4096], P('wsh')
- grad_down_weight: float32 [4096, 1024], P('wsh')
- grad_down_bias: float32 [1024], P('wsh')
Inputs may be any that keep to these rules, and one draw needn't show every extreme that they name: `block_map`: row i lists, in stored order, the blocks b and 15 - b for one b < 8; every block appears exactly once. Each sequence's positions start at 0 and never fall; from one token to the next they rise by 0 or 1, by 1 at exactly (2047) // 8 of the steps.
All inputs are finite; a program needn't handle non-finite values.
Results may differ from a plain program's by a relative error of at most 0.02.
Values may be sent and summed in bfloat16 or wider, within the bound.
A program may use at most 320 MiB of HBM per device.

v0:
```python
import jax
import jax.numpy as jnp
from jax import lax
from jax.sharding import PartitionSpec as P

HEADS = 16


EPS = 1e-05


def for_sending(value):
    return jax.tree.map(lambda a: a.astype(jnp.bfloat16) if a.dtype == jnp.float32 else a, value)


def head_slopes(count):
    return 2.0 ** (-8.0 * (jnp.arange(count, dtype=jnp.float32) + 1.0) / count)


def smooth_gelu(values):
    return jax.nn.gelu(values, approximate=True)


def unchanged(state):
    return state


def norm_forward(values, gain_vec, shift_vec):
    row_mean = jnp.mean(values, axis=-1, keepdims=True)
    centered = values - row_mean
    variance = jnp.mean(centered * centered, axis=-1, keepdims=True)
    inverse = lax.rsqrt(variance + EPS)
    scaled = centered * inverse
    return (scaled * gain_vec + shift_vec, scaled, inverse)


def norm_backward(grad_out, scaled, inverse, gain_vec):
    grad_scaled = grad_out * gain_vec
    mean_grad = jnp.mean(grad_scaled, axis=-1, keepdims=True)
    mean_along = jnp.mean(grad_scaled * scaled, axis=-1, keepdims=True)
    grad_in = inverse * (grad_scaled - mean_grad - scaled * mean_along)
    return (grad_in, jnp.sum(grad_out * scaled, axis=0), jnp.sum(grad_out, axis=0))


def pick_rows(table, order_ids):
    picked = jnp.take(table, order_ids, axis=0)
    return picked.reshape((picked.shape[0] * picked.shape[1],) + picked.shape[2:])


def block_scores(query_heads, query_pos, key_heads, key_pos, slopes):
    score_scale = query_heads.shape[-1] ** (-0.5)
    raw_scores = jnp.einsum(
        "qhd,khd->hqk", query_heads, key_heads, preferred_element_type=jnp.float32
    )
    distance = (query_pos[:, None] - key_pos[None, :]).astype(jnp.float32)
    scores = raw_scores * score_scale - slopes[:, None, None] * distance[None]
    return jnp.where((distance >= 0.0)[None], scores, -jnp.inf)


def online_update(carry, query_heads, query_pos, key_heads, value_heads, key_pos, slopes):
    row_top, row_total, accumulated = carry
    scores = block_scores(query_heads, query_pos, key_heads, key_pos, slopes)
    new_top = jnp.maximum(row_top, jnp.max(scores, axis=-1))
    rescale = jnp.exp(row_top - new_top)
    exponents = jnp.exp(scores - new_top[:, :, None])
    row_total = row_total * rescale + jnp.sum(exponents, axis=-1)
    accumulated = accumulated * rescale.T[:, :, None] + jnp.einsum(
        "hqk,khd->qhd",
        exponents.astype(jnp.bfloat16),
        value_heads,
        preferred_element_type=jnp.float32,
    )
    return (new_top, row_total, accumulated)


def block_grads(
    query_heads, query_pos, key_heads, value_heads, key_pos, slopes, grad_heads, log_total, row_dot
):
    score_scale = query_heads.shape[-1] ** (-0.5)
    scores = block_scores(query_heads, query_pos, key_heads, key_pos, slopes)
    weights_full = jnp.exp(scores - log_total[:, :, None])
    grad_weights = jnp.einsum(
        "qhd,khd->hqk", grad_heads, value_heads, preferred_element_type=jnp.float32
    )
    grad_raw = (weights_full * (grad_weights - row_dot[:, :, None]) * score_scale).astype(
        jnp.bfloat16
    )
    return (grad_raw, weights_full.astype(jnp.bfloat16))


def column_sum(values):
    return jnp.sum(values.astype(jnp.float32), axis=0)


def body(
    tokens,
    block_map,
    positions,
    norm_gain_one,
    norm_shift_one,
    qkv_weight,
    query_bias,
    value_bias,
    dense_weight,
    dense_bias,
    norm_gain_two,
    norm_shift_two,
    up_weight,
    up_bias,
    down_weight,
    down_bias,
    cotangent,
):
    model_width = tokens.shape[2]
    count_tok = tokens.shape[1]
    half_tok = count_tok // 2
    ctx_size = lax.axis_size("ctx")
    block_total = 2 * ctx_size
    head_dim = model_width // HEADS
    slopes = head_slopes(HEADS)
    seq_pos = positions[0]
    stored_ids = block_map.reshape(-1)
    block_ids = jnp.arange(block_total, dtype=jnp.int32)
    seq_order = jnp.sum(
        jnp.where(stored_ids[None, :] == block_ids[:, None], block_ids[None, :], 0), axis=1
    )
    my_blocks = lax.dynamic_index_in_dim(block_map, lax.axis_index("ctx"), 0, keepdims=False)
    my_rows = (
        my_blocks[:, None] * half_tok + jnp.arange(half_tok, dtype=jnp.int32)[None, :]
    ).reshape(-1)
    query_pos = seq_pos[my_rows]
    pos_halves = query_pos.reshape(2, half_tok)
    last_pos = jnp.max(pos_halves, axis=1)
    group_size = min(block_total, max(1, 512 // half_tok))
    group_rows = group_size * half_tok
    group_count = block_total // group_size
    group_parts = (
        seq_order.reshape(group_count, group_size),
        seq_pos.reshape(group_count, group_rows),
    )
    (
        gain_first,
        shift_first,
        qkv_full,
        query_shift,
        value_shift,
        dense_full,
        dense_shift,
        gain_second,
        shift_second,
        up_full,
        up_shift,
        down_full,
        down_shift,
    ) = (
        lax.all_gather(norm_gain_one, "wsh", axis=0, tiled=True),
        lax.all_gather(norm_shift_one, "wsh", axis=0, tiled=True),
        lax.all_gather(qkv_weight, "wsh", axis=0, tiled=True),
        lax.all_gather(query_bias, "wsh", axis=0, tiled=True),
        lax.all_gather(value_bias, "wsh", axis=0, tiled=True),
        lax.all_gather(dense_weight, "wsh", axis=0, tiled=True),
        lax.all_gather(dense_bias, "wsh", axis=0, tiled=True),
        lax.all_gather(norm_gain_two, "wsh", axis=0, tiled=True),
        lax.all_gather(norm_shift_two, "wsh", axis=0, tiled=True),
        lax.all_gather(up_weight, "wsh", axis=0, tiled=True),
        lax.all_gather(up_bias, "wsh", axis=0, tiled=True),
        lax.all_gather(down_weight, "wsh", axis=0, tiled=True),
        lax.all_gather(down_bias, "wsh", axis=0, tiled=True),
    )
    inputs = tokens[0].astype(jnp.float32)
    normed, scaled_first, inverse_first = norm_forward(
        inputs, gain_first.astype(jnp.float32), shift_first.astype(jnp.float32)
    )
    normed_low = normed.astype(jnp.bfloat16)
    mixed = jnp.dot(normed_low, qkv_full, preferred_element_type=jnp.float32)
    query = (mixed[:, :model_width] + query_shift.astype(jnp.float32)).astype(jnp.bfloat16)
    keys_local = mixed[:, model_width : 2 * model_width].astype(jnp.bfloat16)
    values_local = (mixed[:, 2 * model_width :] + value_shift.astype(jnp.float32)).astype(
        jnp.bfloat16
    )
    keys_all, values_all = (
        lax.all_gather(keys_local, "ctx", axis=0, tiled=True),
        lax.all_gather(values_local, "ctx", axis=0, tiled=True),
    )
    key_table = keys_all.reshape(block_total, half_tok, HEADS, head_dim)
    value_table = values_all.reshape(block_total, half_tok, HEADS, head_dim)
    query_halves = query.reshape(2, half_tok, HEADS, head_dim)

    def forward_step(carries, step_parts):
        order_ids, block_pos = step_parts
        key_heads = pick_rows(key_table, order_ids)
        value_heads = pick_rows(value_table, order_ids)
        first_key = jnp.min(block_pos)
        updated = []
        for which_half in range(2):

            def attend(carry, which_half=which_half):
                return online_update(
                    carry,
                    query_halves[which_half],
                    pos_halves[which_half],
                    key_heads,
                    value_heads,
                    block_pos,
                    slopes,
                )

            updated.append(
                lax.cond(first_key <= last_pos[which_half], attend, unchanged, carries[which_half])
            )
        return (tuple(updated), None)

    start_top = jnp.full((HEADS, half_tok), -1e30, jnp.float32)
    start_half = (
        start_top,
        jnp.zeros_like(start_top),
        jnp.zeros((half_tok, HEADS, head_dim), jnp.float32),
    )
    finals = lax.scan(forward_step, (start_half, start_half), group_parts)[0]
    attended = jnp.concatenate(
        [
            summed_values / summed_total.T[:, :, None]
            for final_top, summed_total, summed_values in finals
        ],
        axis=0,
    )
    log_total = jnp.concatenate(
        [final_top + jnp.log(summed_total) for final_top, summed_total, summed_values in finals],
        axis=1,
    )
    attended = attended.reshape(count_tok, model_width)
    context = attended.astype(jnp.bfloat16)
    middle = (
        inputs
        + jnp.dot(context, dense_full, preferred_element_type=jnp.float32)
        + dense_shift.astype(jnp.float32)
    )
    normed_two, scaled_second, inverse_second = norm_forward(
        middle, gain_second.astype(jnp.float32), shift_second.astype(jnp.float32)
    )
    normed_two_low = normed_two.astype(jnp.bfloat16)
    hidden = jnp.dot(normed_two_low, up_full, preferred_element_type=jnp.float32) + up_shift.astype(
        jnp.float32
    )
    activated, gelu_back = jax.vjp(smooth_gelu, hidden)
    active_low = activated.astype(jnp.bfloat16)
    result = (
        middle
        + jnp.dot(active_low, down_full, preferred_element_type=jnp.float32)
        + down_shift.astype(jnp.float32)
    )
    layer_out = result.astype(jnp.bfloat16)[None]
    gain_first, qkv_full, dense_full, gain_second, up_full, down_full = (
        lax.all_gather(norm_gain_one, "wsh", axis=0, tiled=True),
        lax.all_gather(qkv_weight, "wsh", axis=0, tiled=True),
        lax.all_gather(dense_weight, "wsh", axis=0, tiled=True),
        lax.all_gather(norm_gain_two, "wsh", axis=0, tiled=True),
        lax.all_gather(up_weight, "wsh", axis=0, tiled=True),
        lax.all_gather(down_weight, "wsh", axis=0, tiled=True),
    )
    grad_result = cotangent[0].astype(jnp.float32)
    grad_down_low = grad_result.astype(jnp.bfloat16)
    grad_down_weight = jnp.einsum(
        "tf,td->fd", active_low, grad_down_low, preferred_element_type=jnp.float32
    )
    grad_down_shift = column_sum(grad_down_low)
    grad_active = jnp.einsum(
        "td,fd->tf", grad_down_low, down_full, preferred_element_type=jnp.float32
    )
    grad_hidden_low = gelu_back(grad_active)[0].astype(jnp.bfloat16)
    grad_up_shift = column_sum(grad_hidden_low)
    grad_up_weight = jnp.einsum(
        "td,tf->df", normed_two_low, grad_hidden_low, preferred_element_type=jnp.float32
    )
    grad_normed_two = jnp.einsum(
        "tf,df->td", grad_hidden_low, up_full, preferred_element_type=jnp.float32
    )
    grad_middle_part, grad_gain_second, grad_shift_second = norm_backward(
        grad_normed_two, scaled_second, inverse_second, gain_second.astype(jnp.float32)
    )
    grad_middle = grad_result + grad_middle_part
    grad_proj_low = grad_middle.astype(jnp.bfloat16)
    grad_dense_shift = column_sum(grad_proj_low)
    grad_dense_weight = jnp.einsum(
        "td,te->de", context, grad_proj_low, preferred_element_type=jnp.float32
    )
    grad_context_low = jnp.einsum(
        "te,de->td", grad_proj_low, dense_full, preferred_element_type=jnp.float32
    ).astype(jnp.bfloat16)
    grad_heads = grad_context_low.reshape(count_tok, HEADS, head_dim)
    row_dot = jnp.sum(
        grad_heads.astype(jnp.float32) * attended.reshape(count_tok, HEADS, head_dim), axis=-1
    ).T
    grad_halves = grad_heads.reshape(2, half_tok, HEADS, head_dim)
    log_halves = [log_total[:, which * half_tok : (which + 1) * half_tok] for which in range(2)]
    dot_halves = [row_dot[:, which * half_tok : (which + 1) * half_tok] for which in range(2)]
    half_zero = jnp.zeros((half_tok, HEADS, head_dim), jnp.float32)

    def grad_step(carries, step_parts):
        query_pair, key_store, value_store = carries
        order_ids, block_pos = step_parts
        key_heads = pick_rows(key_table, order_ids)
        value_heads = pick_rows(value_table, order_ids)
        first_key = jnp.min(block_pos)
        block_zero = jnp.zeros((group_rows, HEADS, head_dim), jnp.float32)
        keys_block, values_block = (block_zero, block_zero)
        new_pair = []
        for which_half in range(2):

            def backprop(state_in, which_half=which_half):
                grad_query_half, grad_keys_block, grad_values_block = state_in
                grad_raw, weights_low = block_grads(
                    query_halves[which_half],
                    pos_halves[which_half],
                    key_heads,
                    value_heads,
                    block_pos,
                    slopes,
                    grad_halves[which_half],
                    log_halves[which_half],
                    dot_halves[which_half],
                )
                grad_query_half = grad_query_half + jnp.einsum(
                    "hqk,khd->qhd", grad_raw, key_heads, preferred_element_type=jnp.float32
                )
                grad_keys_block = grad_keys_block + jnp.einsum(
                    "hqk,qhd->khd",
                    grad_raw,
                    query_halves[which_half],
                    preferred_element_type=jnp.float32,
                )
                grad_values_block = grad_values_block + jnp.einsum(
                    "hqk,qhd->khd",
                    weights_low,
                    grad_halves[which_half],
                    preferred_element_type=jnp.float32,
                )
                return (grad_query_half, grad_keys_block, grad_values_block)

            grad_query_half, keys_block, values_block = lax.cond(
                first_key <= last_pos[which_half],
                backprop,
                unchanged,
                (query_pair[which_half], keys_block, values_block),
            )
            new_pair.append(grad_query_half)
        key_store = key_store.at[order_ids].set(
            keys_block.reshape(group_size, half_tok, model_width)
        )
        value_store = value_store.at[order_ids].set(
            values_block.reshape(group_size, half_tok, model_width)
        )
        return ((tuple(new_pair), key_store, value_store), None)

    store_zero = jnp.zeros((block_total, half_tok, model_width), jnp.float32)
    query_pair, key_store, value_store = lax.scan(
        grad_step, ((half_zero, half_zero), store_zero, store_zero), group_parts
    )[0]
    grad_query = jnp.concatenate(query_pair, axis=0)
    key_sum, value_sum = (
        lax.psum_scatter(
            key_store.reshape(ctx_size * count_tok, model_width).astype(jnp.bfloat16),
            "ctx",
            scatter_dimension=0,
            tiled=True,
        ).astype(jnp.float32),
        lax.psum_scatter(
            value_store.reshape(ctx_size * count_tok, model_width).astype(jnp.bfloat16),
            "ctx",
            scatter_dimension=0,
            tiled=True,
        ).astype(jnp.float32),
    )
    grad_query_low = grad_query.reshape(count_tok, model_width).astype(jnp.bfloat16)
    grad_value_low = value_sum.astype(jnp.bfloat16)
    grad_mixed = jnp.concatenate(
        [grad_query_low, key_sum.astype(jnp.bfloat16), grad_value_low], axis=1
    )
    grad_query_shift = column_sum(grad_query_low)
    grad_value_shift = column_sum(grad_value_low)
    grad_qkv_weight = jnp.einsum(
        "td,te->de", normed_low, grad_mixed, preferred_element_type=jnp.float32
    )
    grad_normed = jnp.einsum("te,de->td", grad_mixed, qkv_full, preferred_element_type=jnp.float32)
    grad_input_part, grad_gain_first, grad_shift_first = norm_backward(
        grad_normed, scaled_first, inverse_first, gain_first.astype(jnp.float32)
    )
    input_grad = (grad_middle + grad_input_part).astype(jnp.bfloat16)[None]
    owned = (
        lax.psum_scatter(
            grad_gain_first.astype(jnp.bfloat16), "wsh", scatter_dimension=0, tiled=True
        ).astype(jnp.float32),
        lax.psum_scatter(
            grad_shift_first.astype(jnp.bfloat16), "wsh", scatter_dimension=0, tiled=True
        ).astype(jnp.float32),
        lax.psum_scatter(
            grad_qkv_weight.astype(jnp.bfloat16), "wsh", scatter_dimension=0, tiled=True
        ).astype(jnp.float32),
        lax.psum_scatter(
            grad_query_shift.astype(jnp.bfloat16), "wsh", scatter_dimension=0, tiled=True
        ).astype(jnp.float32),
        lax.psum_scatter(
            grad_value_shift.astype(jnp.bfloat16), "wsh", scatter_dimension=0, tiled=True
        ).astype(jnp.float32),
        lax.psum_scatter(
            grad_dense_weight.astype(jnp.bfloat16), "wsh", scatter_dimension=0, tiled=True
        ).astype(jnp.float32),
        lax.psum_scatter(
            grad_dense_shift.astype(jnp.bfloat16), "wsh", scatter_dimension=0, tiled=True
        ).astype(jnp.float32),
        lax.psum_scatter(
            grad_gain_second.astype(jnp.bfloat16), "wsh", scatter_dimension=0, tiled=True
        ).astype(jnp.float32),
        lax.psum_scatter(
            grad_shift_second.astype(jnp.bfloat16), "wsh", scatter_dimension=0, tiled=True
        ).astype(jnp.float32),
        lax.psum_scatter(
            grad_up_weight.astype(jnp.bfloat16), "wsh", scatter_dimension=0, tiled=True
        ).astype(jnp.float32),
        lax.psum_scatter(
            grad_up_shift.astype(jnp.bfloat16), "wsh", scatter_dimension=0, tiled=True
        ).astype(jnp.float32),
        lax.psum_scatter(
            grad_down_weight.astype(jnp.bfloat16), "wsh", scatter_dimension=0, tiled=True
        ).astype(jnp.float32),
        lax.psum_scatter(
            grad_down_shift.astype(jnp.bfloat16), "wsh", scatter_dimension=0, tiled=True
        ).astype(jnp.float32),
    )
    summed = jax.tree.map(
        lambda part: part.astype(jnp.float32), lax.psum(for_sending(tuple(owned)), "ctx")
    )
    return (layer_out, input_grad) + tuple(summed)


def solution(mesh):
    in_specs = (
        P("wsh", "ctx", None),
        P(),
        P("wsh", None),
        P("wsh"),
        P("wsh"),
        P("wsh", None),
        P("wsh"),
        P("wsh"),
        P("wsh", None),
        P("wsh"),
        P("wsh"),
        P("wsh"),
        P("wsh", None),
        P("wsh"),
        P("wsh", None),
        P("wsh"),
        P("wsh", "ctx", None),
    )
    out_specs = (
        P("wsh", "ctx", None),
        P("wsh", "ctx", None),
        P("wsh"),
        P("wsh"),
        P("wsh", None),
        P("wsh"),
        P("wsh"),
        P("wsh", None),
        P("wsh"),
        P("wsh"),
        P("wsh"),
        P("wsh", None),
        P("wsh"),
        P("wsh", None),
        P("wsh"),
    )
    return jax.shard_map(body, mesh=mesh, in_specs=in_specs, out_specs=out_specs, check_vma=False)
```

profile of v0, /device:TPU:0, one launch (start us, length us, event | category | flops | bytes accessed | tf_op | source)
XLA Modules:
  0.0 1310.5 jit_solution(18439374029383097194)
XLA Ops:
  23.4 35.3 %all-gather.15.cloned.1.call-done = bf16[1024,3072]{1,0:T(8,128)(2,1)} async-done(((bf16[256,3072]{1,0:T(8,128)(2,1)}), bf16[1024,3072]{1,0:T(8,128)(2,1)}) %all-gather.15.cloned.1.call-update) | async-done | bytes 6291472 | tf_op jit(solution)/shard_map/all_gather | solution.py:158
  103.6 34.5 %all-gather.17.cloned.1.call-done = bf16[2048,1024]{1,0:T(8,128)(2,1)} async-done(((bf16[256,1024]{1,0:T(8,128)(2,1)}), bf16[2048,1024]{1,0:T(8,128)(2,1)}) %all-gather.17.cloned.1.call-update) | async-done | bytes 4194320 | tf_op jit(solution)/shard_map/all_gather | solution.py:182
  138.1 11.7 reshape.576
  149.8 62.7 %all-gather.19.cloned.1.call-done = bf16[2048,1024]{1,0:T(8,128)(2,1)} async-done(((bf16[256,1024]{1,0:T(8,128)(2,1)}), bf16[2048,1024]{1,0:T(8,128)(2,1)}) %all-gather.19.cloned.1.call-update) | async-done | bytes 4194320 | tf_op jit(solution)/shard_map/all_gather | solution.py:183
  212.5 11.7 reshape.577
  225.9 137.1 %while.43 = (s32[]{:T(128)}, f32[16,128]{1,0:T(8,128)S(1)}, f32[16,128]{1,0:T(8,128)S(1)}, f32[128,16,64]{0,2,1:T(8,128)}, f32[16,128]{1,0:T(8,128)S(1)}, /*inde...) while((s32[]{:T(128)}, f32[16,128]{1,0:T(8,128)S(1)}, ...), condition=%wide.region_14.16_spmd.clone.clone, body=%wide.region_4.15_spmd.clone.clone.sunk | while | flops 574764608 | bytes 64247816 | solution.py:219
  251.4 6.1 conditional.16
  257.5 6.1 conditional.17
  289.0 6.1 conditional.16
  295.1 6.1 conditional.17
  305.9 6.8 gather_fusion.1
  368.2 7.9 convolution_add_fusion
  376.1 12.1 fusion.129
  410.6 217.7 %while.44 = (s32[]{:T(128)}, f32[128,16,64]{0,2,1:T(8,128)}, f32[128,16,64]{0,2,1:T(8,128)}, f32[16,128,1024]{2,1,0:T(8,128)}, f32[16,128,1024]{2,1,0:T(8,128)},...) while((s32[]{:T(128)}, f32[128,16,64]{0,2,1:T(8,128)}, ...), condition=%wide.region_28.30_spmd.clone.clone, body=%wide.region_20.29_spmd.clone.clone.sunk | while | flops 1376650752 | bytes 134159376 | solution.py:356
  434.7 8.5 conditional.18
  443.2 10.7 conditional.19
  495.2 8.5 conditional.18
  503.6 10.7 conditional.19
  557.3 10.8 conditional.19
  628.3 6.1 convert_element_type.303
  644.0 8.4 convolution_convert_fusion
  653.6 7.3 convolution_convert_fusion.1
  664.3 73.1 %reduce-scatter.9.cloned.1.call-done = bf16[256,1024]{1,0:T(8,128)(2,1)} async-done(((bf16[2048,1024]{1,0:T(8,128)(2,1)}), bf16[256,1024]{1,0:T(8,128)(2,1)}) %reduce-scatter.9.cloned.1.call-update) | async-done | bytes 524304 | tf_op jit(solution)/shard_map/reduce_scatter | solution.py:367
  737.4 91.9 %reduce-scatter.7.cloned.1.call-done = bf16[256,1024]{1,0:T(8,128)(2,1)} async-done(((bf16[2048,1024]{1,0:T(8,128)(2,1)}), bf16[256,1024]{1,0:T(8,128)(2,1)}) %reduce-scatter.7.cloned.1.call-update) | async-done | bytes 524304 | tf_op jit(solution)/shard_map/reduce_scatter | solution.py:361
  835.5 28.2 %reduce-scatter.13.cloned.1.call-done = bf16[256,1024]{1,0:T(8,128)(2,1)} async-done(((bf16[1024,1024]{1,0:T(8,128)(2,1)}), bf16[256,1024]{1,0:T(8,128)(2,1)}) %reduce-scatter.13.cloned.1.call-update) | async-done | bytes 524304 | tf_op jit(solution)/shard_map/reduce_scatter | solution.py:405
  863.6 74.3 %reduce-scatter.17.cloned.1.call-done = bf16[1024,1024]{1,0:T(8,128)(2,1)} async-done(((bf16[4096,1024]{1,0:T(8,128)(2,1)}), bf16[1024,1024]{1,0:T(8,128)(2,1)}) %reduce-scatter.17.cloned.1.call-update) | async-done | bytes 2097168 | tf_op jit(solution)/shard_map/reduce_scatter | solution.py:423
  938.0 74.3 %reduce-scatter.15.cloned.1.call-done = bf16[256,4096]{1,0:T(8,128)(2,1)} async-done(((bf16[1024,4096]{1,0:T(8,128)(2,1)}), bf16[256,4096]{1,0:T(8,128)(2,1)}) %reduce-scatter.15.cloned.1.call-update) | async-done | bytes 2097168 | tf_op jit(solution)/shard_map/reduce_scatter | solution.py:417
  1012.3 61.0 %reduce-scatter.11.cloned.1.call-done = bf16[256,3072]{1,0:T(8,128)(2,1)} async-done(((bf16[1024,3072]{1,0:T(8,128)(2,1)}), bf16[256,3072]{1,0:T(8,128)(2,1)}) %reduce-scatter.11.cloned.1.call-update) | async-done | bytes 1572880 | tf_op jit(solution)/shard_map/reduce_scatter | solution.py:396
  1080.8 9.0 fusion.95
  1095.5 11.2 all-reduce.11
  1107.3 22.9 %all-reduce.9 = (bf16[256]{0:T(256)(128)(2,1)S(1)}, bf16[256]{0:T(256)(128)(2,1)S(1)}, bf16[256]{0:T(256)(128)(2,1)S(1)}, bf16[256]{0:T(256)(128)(2,1)S(1)}, bf1...) all-reduce(bf16[256]{0:T(256)(128)(2,1)S(1)} %dynamic-slice.1, ...), channel_id=1, replica_groups=mesh['ctx'=8,'wsh'=4] {'ctx'}, use_global_device_ids=true, to_apply=%region_35.37 | all-reduce | flops 3072 | bytes 12288 | tf_op jit(solution)/shard_map/psum | solution.py:431
  1136.5 156.3 %all-reduce.14.cloned.1.call-done = (bf16[256,3072]{1,0:T(8,128)(2,1)}, bf16[256,1024]{1,0:T(8,128)(2,1)}, bf16[256,4096]{1,0:T(8,128)(2,1)}, bf16[1024,1024]{1,0:T(8,128)(2,1)}) async-done(((bf16[256,3072]{1,0:T(8,128)(2,1)}, bf16[256,1024]{1,0:T(8,128)(2,1)}, bf16[256,4096]{1,0:T(8,128)(2,1)}, bf16[1024,1024]{1,0:T(8,128)(2,1)}), (bf16[256,3072]{1,0:T(8,128)(2,1)}, bf16[256,1024]{1,0:T(8,128)(2,1)}, ...) | async-done | bytes 6291472 | tf_op jit(solution)/shard_map/psum | solution.py:431
  (552 shorter events, 474.2 us)
Async XLA Ops:
  7.2 51.5 %all-gather.15.cloned.1.call-start = ((), (), s32[]{:S(2)}) async-start(), calls=%async_computation.6 | async-start | bytes 7864320 | tf_op jit(solution)/shard_map/all_gather | solution.py:158
  7.9 130.2 %all-gather.17.cloned.1.call-start = ((), (), s32[]{:S(2)}) async-start(), calls=%async_computation.7 | async-start | bytes 4718592 | tf_op jit(solution)/shard_map/all_gather | solution.py:182
  15.3 48.3 %copy-start.60 = (f32[4,1,256]{2,1,0:T(1,128)}, f32[4,1,256]{2,1,0:T(1,128)S(1)}, u32[]{:S(2)}) copy-start(f32[4,1,256]{2,1,0:T(1,128)S(1)} %convert_element_type.333) | copy-start | bytes 12292
  20.6 43.0 %copy-start.51 = (f32[4,1,256]{2,1,0:T(1,128)}, f32[4,1,256]{2,1,0:T(1,128)S(1)}, u32[]{:S(2)}) copy-start(f32[4,1,256]{2,1,0:T(1,128)S(1)} %convert_element_type.332) | copy-start | bytes 12292
  22.0 41.6 %copy-start.53 = (f32[256]{0:T(256)}, f32[256]{0:T(256)S(1)}, u32[]{:S(2)}) copy-start(f32[256]{0:T(256)S(1)} %broadcast_multiply_fusion.5) | copy-start | bytes 3076
  23.4 40.3 %copy-start.57 = (f32[256]{0:T(256)}, f32[256]{0:T(256)S(1)}, u32[]{:S(2)}) copy-start(f32[256]{0:T(256)S(1)} %add_rsqrt_fusion.1) | copy-start | bytes 3076
  64.5 148.0 %all-gather.19.cloned.1.call-start = ((), (), s32[]{:S(2)}) async-start(), calls=%async_computation.8 | async-start | bytes 4718592 | tf_op jit(solution)/shard_map/all_gather | solution.py:183
  76.1 26.0 %copy-start.36 = (bf16[256,1024]{1,0:T(8,128)(2,1)S(1)}, bf16[256,1024]{1,0:T(8,128)(2,1)}, u32[]{:S(2)}) copy-start(bf16[256,1024]{1,0:T(8,128)(2,1)} %get-tuple-element.792) | copy-start | bytes 1572868
  76.1 289.1 %all-gather.21.cloned.1.call-start = ((), (), s32[]{:S(2)}) async-start(), calls=%async_computation.9 | async-start | bytes 2621440 | tf_op jit(solution)/shard_map/all_gather | solution.py:161
  76.7 291.5 %all-gather.23.cloned.1.call-start = ((), (), s32[]{:S(2)}) async-start(), calls=%async_computation.10 | async-start | bytes 10485760 | tf_op jit(solution)/shard_map/all_gather | solution.py:165
  77.2 298.8 %all-gather.25.cloned.1.call-start = ((), (), s32[]{:S(2)}) async-start(), calls=%async_computation.11 | async-start | bytes 10485760 | tf_op jit(solution)/shard_map/all_gather | solution.py:167
  77.8 659.6 %reduce-scatter.9.cloned.1.call-start = ((), (), s32[]{:S(2)}) async-start(), calls=%async_computation.13 | async-start | bytes 4718592 | tf_op jit(solution)/shard_map/reduce_scatter | solution.py:367
  83.0 285.1 %copy-start.45 = (f32[4,1,256]{2,1,0:T(1,128)}, f32[4,1,256]{2,1,0:T(1,128)S(1)}, u32[]{:S(2)}) copy-start(f32[4,1,256]{2,1,0:T(1,128)S(1)} %convert_element_type.338) | copy-start | bytes 12292
  88.1 303.3 %copy-start.43 = (f32[4,1,256]{2,1,0:T(1,128)}, f32[4,1,256]{2,1,0:T(1,128)S(1)}, u32[]{:S(2)}) copy-start(f32[4,1,256]{2,1,0:T(1,128)S(1)} %convert_element_type.337) | copy-start | bytes 12292
  225.9 139.3 %copy-start.20 = (bf16[1,256,1024]{2,1,0:T(8,128)(2,1)S(1)}, bf16[1,256,1024]{2,1,0:T(8,128)(2,1)}, u32[]{:S(2)}) copy-start(bf16[1,256,1024]{2,1,0:T(8,128)(2,1)} %param.31) | copy-start | bytes 1572868
  367.8 23.6 %copy-start.15 = (f32[256,1024]{1,0:T(8,128)}, f32[256,1024]{1,0:T(8,128)S(1)}, u32[]{:S(2)}) copy-start(f32[256,1024]{1,0:T(8,128)S(1)} %get-tuple-element.797) | copy-start | bytes 3145732
  367.8 23.6 %copy-start.47 = (f32[256]{0:T(256)}, f32[256]{0:T(256)S(1)}, u32[]{:S(2)}) copy-start(f32[256]{0:T(256)S(1)} %broadcast_multiply_fusion.4) | copy-start | bytes 3076
  368.1 23.3 %copy-start.49 = (f32[256]{0:T(256)}, f32[256]{0:T(256)S(1)}, u32[]{:S(2)}) copy-start(f32[256]{0:T(256)S(1)} %add_rsqrt_fusion) | copy-start | bytes 3076
  634.4 194.9 %reduce-scatter.7.cloned.1.call-start = ((), (), s32[]{:S(2)}) async-start(), calls=%async_computation.12 | async-start | bytes 4718592 | tf_op jit(solution)/shard_map/reduce_scatter | solution.py:361
  640.5 223.1 %reduce-scatter.13.cloned.1.call-start = ((), (), s32[]{:S(2)}) async-start(), calls=%async_computation.15 | async-start | bytes 2621440 | tf_op jit(solution)/shard_map/reduce_scatter | solution.py:405
  643.9 294.1 %reduce-scatter.17.cloned.1.call-start = ((), (), s32[]{:S(2)}) async-start(), calls=%async_computation.17 | async-start | bytes 10485760 | tf_op jit(solution)/shard_map/reduce_scatter | solution.py:423
  652.4 359.9 %reduce-scatter.15.cloned.1.call-start = ((), (), s32[]{:S(2)}) async-start(), calls=%async_computation.16 | async-start | bytes 10485760 | tf_op jit(solution)/shard_map/reduce_scatter | solution.py:417
  660.9 168.4 %copy-start.52 = (f32[4,1,256]{2,1,0:T(1,128)S(1)}, f32[4,1,256]{2,1,0:T(1,128)}, u32[]{:S(2)}) copy-start(f32[4,1,256]{2,1,0:T(1,128)} %copy-done.51) | copy-start | bytes 12292
  660.9 168.4 %copy-start.54 = (f32[256]{0:T(256)S(1)}, f32[256]{0:T(256)}, u32[]{:S(2)}) copy-start(f32[256]{0:T(256)} %copy-done.53) | copy-start | bytes 3076
  660.9 168.4 %copy-start.58 = (f32[256]{0:T(256)S(1)}, f32[256]{0:T(256)}, u32[]{:S(2)}) copy-start(f32[256]{0:T(256)} %copy-done.57) | copy-start | bytes 3076
  660.9 168.4 %copy-start.61 = (f32[4,1,256]{2,1,0:T(1,128)S(1)}, f32[4,1,256]{2,1,0:T(1,128)}, u32[]{:S(2)}) copy-start(f32[4,1,256]{2,1,0:T(1,128)} %copy-done.60) | copy-start | bytes 12292
  661.0 412.3 %reduce-scatter.11.cloned.1.call-start = ((), (), s32[]{:S(2)}) async-start(), calls=%async_computation.14 | async-start | bytes 7864320 | tf_op jit(solution)/shard_map/reduce_scatter | solution.py:396
  664.3 171.1 %copy-start.42 = (bf16[256,1024]{1,0:T(8,128)(2,1)}, bf16[256,1024]{1,0:T(8,128)(2,1)S(1)}, u32[]{:S(2)}) copy-start(bf16[256,1024]{1,0:T(8,128)(2,1)S(1)} %copy.103) | copy-start | bytes 1572868
  835.4 237.9 %copy-start.72 = (u32[32]{0:T(128)S(1)}, u32[32]{0:T(128)}, u32[]{:S(2)}) copy-start(u32[32]{0:T(128)} %constant.131) | copy-start | bytes 388
  835.4 239.8 %copy-start.71 = (bf16[256]{0:T(256)(128)(2,1)S(1)}, bf16[256]{0:T(256)(128)(2,1)}, u32[]{:S(2)}) copy-start(bf16[256]{0:T(256)(128)(2,1)} %param.46) | copy-start | bytes 1540
  835.4 239.8 %copy-start.35 = (bf16[1,256,1024]{2,1,0:T(8,128)(2,1)S(1)}, bf16[1,256,1024]{2,1,0:T(8,128)(2,1)}, u32[]{:S(2)}) copy-start(bf16[1,256,1024]{2,1,0:T(8,128)(2,1)} %param.47) | copy-start | bytes 1572868
  835.4 457.4 %all-reduce.14.cloned.1.call-start = ((), (), s32[]{:S(2)}) async-start(), calls=%async_computation.18 | async-start | bytes 12582912 | tf_op jit(solution)/shard_map/psum | solution.py:431
  (86 other events, 371.1 us)
Sparse Core Ops, SparseCore 0:
  9.6 49.0 all-gather.14
  64.6 73.3 all-gather.16
  140.8 71.6 all-gather.18
  213.9 20.8 all-gather.20
  236.2 58.2 all-gather.22
  295.9 58.2 all-gather.24
  634.5 102.7 reduce-scatter.8
  741.4 87.8 reduce-scatter.6
  832.4 31.1 reduce-scatter.12
  866.2 71.6 reduce-scatter.16
  940.5 71.7 reduce-scatter.14
  1014.8 58.3 reduce-scatter.10
  1077.7 215.0 all-reduce.13
where the time goes:
time: 1320 us; the launch traced here: 1310 us
  waiting for transfers between devices  694 us (53%)
  local copies, waits for them, and re-layouts  274 us (21%)
  matrix products  134 us (10%)
  other arithmetic  87.4 us (7%)
  blocking collectives  81.3 us (6%)
  loops' own time  23 us (2%)
  between operations  16.3 us (1%)
    psum x1, waiting for transfers between devices, body(): lax.psum(for_sending(tuple(owned)), 'ctx')  156 us
    reduce_scatter x1, waiting for transfers between devices, body(): lax.psum_scatter(key_store.reshape(ctx_size * count_tok, model_width).ast...  91.9 us
    gather x16, local copies, waits for them, and re-layouts, pick_rows(): picked = jnp.take(table, order_ids, axis=0)  89.8 us
    reduce_scatter x1, waiting for transfers between devices, body(): lax.psum_scatter(grad_up_weight.astype(jnp.bfloat16), 'wsh', scatter_dime...  74.3 us
    reduce_scatter x1, waiting for transfers between devices, body(): lax.psum_scatter(grad_down_weight.astype(jnp.bfloat16), 'wsh', scatter_di...  74.3 us
    reduce_scatter x1, waiting for transfers between devices, body(): lax.psum_scatter(value_store.reshape(ctx_size * count_tok, model_width).a...  73.1 us
    all_gather x1, waiting for transfers between devices, body(): lax.all_gather(values_local, 'ctx', axis=0, tiled=True)  62.7 us
    reduce_scatter x1, waiting for transfers between devices, body(): lax.psum_scatter(grad_qkv_weight.astype(jnp.bfloat16), 'wsh', scatter_dim...  61 us
  transfers between devices with their start and end apart: 13, of which 10 were waited for; matrix products, arithmetic and copies ran while one was open for 17% of the time, Pallas kernels for 0%

commit v1 on v0

v1 whole, which is shorter than its diff:
```python
import functools

import jax
import jax.numpy as jnp
from jax import lax
from jax.experimental import pallas as pl
from jax.experimental.pallas import tpu as pltpu
from jax.sharding import PartitionSpec as P

HEADS = 16
EPS = 1e-05
LANES = 128
QUERY_TILE = 256
KEY_TILE = 512
FAR = -1e30
F32 = jnp.float32
BF16 = jnp.bfloat16


def norm_forward(values, gain_vec, shift_vec):
    row_mean = jnp.mean(values, axis=-1, keepdims=True)
    centered = values - row_mean
    variance = jnp.mean(centered * centered, axis=-1, keepdims=True)
    inverse = lax.rsqrt(variance + EPS)
    scaled = centered * inverse
    return (scaled * gain_vec + shift_vec, scaled, inverse)


def norm_backward(grad_out, scaled, inverse, gain_vec):
    grad_scaled = grad_out * gain_vec
    mean_grad = jnp.mean(grad_scaled, axis=-1, keepdims=True)
    mean_along = jnp.mean(grad_scaled * scaled, axis=-1, keepdims=True)
    grad_in = inverse * (grad_scaled - mean_grad - scaled * mean_along)
    return (grad_in, jnp.sum(grad_out * scaled, axis=0), jnp.sum(grad_out, axis=0))


def gelu_tanh(values):
    return jax.nn.gelu(values, approximate=True)


def dot(a, b, dims):
    return lax.dot_general(a, b, (dims, ((), ())), preferred_element_type=F32)


def column_sum(values):
    return jnp.sum(values.astype(F32), axis=0)


def slot_rows(order_ref, step, rows, first):
    slot = order_ref[step]
    src = slot // 2
    return src, pl.ds(pl.multiple_of(first + (slot % 2) * rows, 16), rows)


def split_heads(tile):
    lane = lax.broadcasted_iota(jnp.int32, tile.shape, 1)
    zero = jnp.zeros_like(tile)
    half = LANES // 2
    return (jnp.where(lane < half, tile, zero), jnp.where(lane >= half, tile, zero))


def load_sequence(query_block, half_tok, order_ref, packed_ref, q_s, k_s, v_s):
    first_key = 2 * query_block
    first_value = first_key + 2 * half_tok

    def load(step, _):
        src, rows = slot_rows(order_ref, step, query_block, 0)
        to = pl.ds(pl.multiple_of(step * query_block, 16), query_block)
        q_s[to, :] = packed_ref[src, rows, :]
        to = pl.ds(pl.multiple_of(step * half_tok, 16), half_tok)
        src, rows = slot_rows(order_ref, step, half_tok, first_key)
        k_s[to, :] = packed_ref[src, rows, :]
        src, rows = slot_rows(order_ref, step, half_tok, first_value)
        v_s[to, :] = packed_ref[src, rows, :]
        return 0

    lax.fori_loop(0, order_ref.shape[0], load, 0)


def transpose_into(to_ref, from_ref, key_tile):
    def turn(step, _):
        rows = pl.ds(pl.multiple_of(step * key_tile, key_tile), key_tile)
        to_ref[:, rows] = from_ref[rows, :].astype(F32).T.astype(BF16)
        return 0

    lax.fori_loop(0, from_ref.shape[0] // key_tile, turn, 0)


def tile_bias(key_pos_ref, keys, query_pos):
    distance = key_pos_ref[keys, :] - query_pos
    return jnp.where(distance <= 0.0, distance, FAR)


def forward_kernel(
    query_block, half_tok, query_tile, key_tile,
    order_ref, count_ref, slope_ref, packed_ref, query_pos_ref, key_pos_ref,
    context_ref, attended_ref, log_ref, q_s, k_s, v_s, vt_s,
):
    load_sequence(query_block, half_tok, order_ref, packed_ref, q_s, k_s, v_s)
    transpose_into(vt_s, v_s, key_tile)
    half = LANES // 2

    def query_step(qi, _):
        queries = pl.ds(pl.multiple_of(qi * query_tile, query_tile), query_tile)
        q_parts = split_heads(q_s[queries, :] * 0.125)
        query_pos = query_pos_ref[:, queries]

        def key_step(kj, carry):
            keys = pl.ds(pl.multiple_of(kj * key_tile, key_tile), key_tile)
            k_tile = k_s[keys, :]
            bias = tile_bias(key_pos_ref, keys, query_pos)
            out = []
            for h in range(2):
                top, total, acc = carry[h]
                scores = dot(k_tile, q_parts[h], ((1,), (1,))) + slope_ref[h] * bias
                new_top = jnp.maximum(top, jnp.max(scores, axis=0, keepdims=True))
                rescale = jnp.exp(top - new_top)
                weights = jnp.exp(scores - new_top)
                total = total * rescale + jnp.sum(weights, axis=0, keepdims=True)
                v_tile = vt_s[h * half : (h + 1) * half, keys]
                acc = acc * rescale + dot(v_tile, weights.astype(BF16), ((1,), (0,)))
                out.append((new_top, total, acc))
            return tuple(out)

        row = jnp.zeros((1, query_tile), F32)
        start = (row + FAR, row, jnp.zeros((half, query_tile), F32))
        ends = lax.fori_loop(0, count_ref[qi], key_step, (start, start))
        for h in range(2):
            top, total, acc = ends[h]
            attended_ref[h * half : (h + 1) * half, queries] = acc / total
            log_ref[h : h + 1, queries] = top + jnp.log(total)
        q_s[queries, :] = attended_ref[:, queries].T.astype(BF16)
        return 0

    lax.fori_loop(0, q_s.shape[0] // query_tile, query_step, 0)

    def put(step, _):
        src, rows = slot_rows(order_ref, step, query_block, 0)
        at = pl.ds(pl.multiple_of(step * query_block, 16), query_block)
        context_ref[src, rows, :] = q_s[at, :]
        return 0

    lax.fori_loop(0, order_ref.shape[0], put, 0)


def backward_kernel(
    query_block, half_tok, query_tile, key_tile,
    order_ref, count_ref, slope_ref, packed_ref, query_pos_ref, key_pos_ref,
    attended_ref, log_ref, grad_ref,
    out_ref, q_s, k_s, v_s, kt_s, g_s, gk_s, gv_s,
):
    load_sequence(query_block, half_tok, order_ref, packed_ref, q_s, k_s, v_s)
    transpose_into(kt_s, k_s, key_tile)
    half = LANES // 2

    def load(step, _):
        src, rows = slot_rows(order_ref, step, query_block, 0)
        at = pl.ds(pl.multiple_of(step * query_block, 16), query_block)
        g_s[at, :] = grad_ref[src, rows, :]
        return 0

    lax.fori_loop(0, order_ref.shape[0], load, 0)
    gk_s[...] = jnp.zeros_like(gk_s)
    gv_s[...] = jnp.zeros_like(gv_s)

    def query_step(qi, _):
        queries = pl.ds(pl.multiple_of(qi * query_tile, query_tile), query_tile)
        q_parts = split_heads(q_s[queries, :] * 0.125)
        g_tile = g_s[queries, :]
        g_parts = split_heads(g_tile)
        along = g_tile.astype(F32).T * attended_ref[:, queries]
        deltas = [
            jnp.sum(along[h * half : (h + 1) * half], axis=0, keepdims=True) for h in range(2)
        ]
        query_pos = query_pos_ref[:, queries]

        def key_step(kj, carry):
            keys = pl.ds(pl.multiple_of(kj * key_tile, key_tile), key_tile)
            k_tile, v_tile = k_s[keys, :], v_s[keys, :]
            bias = tile_bias(key_pos_ref, keys, query_pos)
            out = []
            add_k, add_v = gk_s[keys, :], gv_s[keys, :]
            for h in range(2):
                scores = dot(k_tile, q_parts[h], ((1,), (1,))) + slope_ref[h] * bias
                weights = jnp.exp(scores - log_ref[h : h + 1, queries])
                grads = dot(v_tile, g_parts[h], ((1,), (1,)))
                raw = (weights * (grads - deltas[h])).astype(BF16)
                add_v = add_v + dot(weights.astype(BF16), g_parts[h], ((1,), (0,)))
                add_k = add_k + dot(raw, q_parts[h], ((1,), (0,)))
                out.append(carry[h] + dot(kt_s[h * half : (h + 1) * half, keys], raw, ((1,), (0,))))
            gk_s[keys, :] = add_k
            gv_s[keys, :] = add_v
            return tuple(out)

        start = jnp.zeros((half, query_tile), F32)
        ends = lax.fori_loop(0, count_ref[qi], key_step, (start, start))
        grad_q = jnp.concatenate(ends, axis=0) * 0.125
        q_s[queries, :] = grad_q.T.astype(BF16)
        return 0

    lax.fori_loop(0, q_s.shape[0] // query_tile, query_step, 0)
    first_key = 2 * query_block
    first_value = first_key + 2 * half_tok

    def put(step, _):
        src, rows = slot_rows(order_ref, step, query_block, 0)
        at = pl.ds(pl.multiple_of(step * query_block, 16), query_block)
        out_ref[src, rows, :] = q_s[at, :]
        at = pl.ds(pl.multiple_of(step * half_tok, 16), half_tok)
        src, rows = slot_rows(order_ref, step, half_tok, first_key)
        out_ref[src, rows, :] = gk_s[at, :].astype(BF16)
        src, rows = slot_rows(order_ref, step, half_tok, first_value)
        out_ref[src, rows, :] = gv_s[at, :].astype(BF16)
        return 0

    lax.fori_loop(0, order_ref.shape[0], put, 0)


def call_local(kernel, outs, scratch, flops, *args):
    smem = pl.BlockSpec(memory_space=pltpu.SMEM)
    vmem = pl.BlockSpec(memory_space=pltpu.VMEM)
    return pl.pallas_call(
        kernel,
        out_shape=outs,
        in_specs=[smem] * 3 + [vmem] * (len(args) - 3),
        out_specs=[vmem] * len(outs),
        scratch_shapes=scratch,
        cost_estimate=pl.CostEstimate(flops=flops, bytes_accessed=6_000_000, transcendentals=flops // 256),
        compiler_params=pltpu.CompilerParams(vmem_limit_bytes=48 * 1024 * 1024),
    )(*args)


def body(
    tokens, block_map, positions, norm_gain_one, norm_shift_one, qkv_weight, query_bias,
    value_bias, dense_weight, dense_bias, norm_gain_two, norm_shift_two, up_weight, up_bias,
    down_weight, down_bias, cotangent,
):
    width = tokens.shape[2]
    count_tok = tokens.shape[1]
    half_tok = count_tok // 2
    ctx = lax.axis_size("ctx")
    wsh = lax.axis_size("wsh")
    blocks = 2 * ctx
    length = ctx * count_tok
    own = width // wsh
    pairs = own // LANES
    units = wsh * pairs
    share = max(1, ctx // units)
    query_block = half_tok // share
    query_count = length // share
    query_tile = min(QUERY_TILE, query_count)
    key_tile = min(KEY_TILE, length)
    all_tok = wsh * count_tok

    def gather(value):
        return lax.all_gather(value, "wsh", axis=0, tiled=True)

    def scatter(value):
        return lax.psum_scatter(value, "wsh", scatter_dimension=0, tiled=True)

    def swap_ctx(value):
        return lax.all_to_all(value, "ctx", split_axis=0, concat_axis=0, tiled=True)

    vectors = jnp.stack(
        [norm_gain_one, norm_shift_one, dense_bias, norm_gain_two, norm_shift_two, down_bias]
    )
    vectors = lax.all_gather(vectors, "wsh", axis=1, tiled=True).astype(F32)
    gain_first, shift_first, dense_shift, gain_second, shift_second, down_shift = vectors
    all_pos = gather(positions)
    qkv_own = lax.all_to_all(
        qkv_weight.reshape(own, 3, wsh, own), "wsh", split_axis=2, concat_axis=0, tiled=True
    ).reshape(width, 3 * own)
    hidden_own = up_weight.shape[1] // wsh
    up_own = lax.all_to_all(
        up_weight.reshape(own, wsh, hidden_own), "wsh", split_axis=1, concat_axis=0, tiled=True
    ).reshape(width, hidden_own)

    unit = lax.axis_index("ctx") // share
    part = lax.axis_index("ctx") % share
    seq_pos = lax.dynamic_index_in_dim(all_pos, unit // pairs, 0, keepdims=False)
    stored = block_map.reshape(-1)
    ids = jnp.arange(blocks, dtype=jnp.int32)
    order = jnp.sum(jnp.where(stored[None, :] == ids[:, None], ids[None, :], 0), axis=1)
    query_pos = lax.dynamic_index_in_dim(
        seq_pos.reshape(blocks, share, query_block), part, 1, keepdims=False
    ).reshape(query_count)
    last_pos = query_pos.reshape(-1, query_tile)[:, -1]
    first_pos = seq_pos.reshape(-1, key_tile)[:, 0]
    counts = jnp.sum((first_pos[None, :] <= last_pos[:, None]).astype(jnp.int32), axis=1)
    head_ids = lax.axis_index("wsh") * (HEADS // wsh) + (unit % pairs) * 2 + jnp.arange(2)
    slopes = 2.0 ** (-8.0 * (head_ids.astype(F32) + 1.0) / HEADS)
    query_row = query_pos.astype(F32).reshape(1, query_count)
    key_column = seq_pos.astype(F32).reshape(length, 1)

    def to_query_units(value):
        shaped = value.reshape(wsh, 2, share, query_block, pairs, LANES)
        return shaped.transpose(0, 4, 2, 1, 3, 5).reshape(ctx, 2 * query_block, LANES)

    def from_query_units(value):
        shaped = value.reshape(wsh, pairs, share, 2, query_block, LANES)
        return shaped.transpose(0, 3, 2, 4, 1, 5).reshape(all_tok, own)

    def to_key_units(value):
        shaped = value.reshape(wsh, count_tok, pairs, LANES).transpose(0, 2, 1, 3)
        shaped = jnp.broadcast_to(shaped[:, :, None], (wsh, pairs, share, count_tok, LANES))
        return shaped.reshape(ctx, count_tok, LANES)

    def from_key_units(value):
        shaped = value.reshape(wsh, pairs, share, count_tok, LANES)
        if share == 1:
            shaped = shaped[:, :, 0]
        else:
            shaped = jnp.sum(shaped.astype(F32), axis=2).astype(BF16)
        return shaped.transpose(0, 2, 1, 3).reshape(all_tok, own)

    inputs = tokens[0].astype(F32)
    normed, scaled_first, inverse_first = norm_forward(inputs, gain_first, shift_first)
    normed_all = gather(normed.astype(BF16))
    grad_all = gather(cotangent[0])
    mixed = jnp.dot(normed_all, qkv_own, preferred_element_type=F32)
    query = (mixed[:, :own] + query_bias.astype(F32)).astype(BF16)
    keys = mixed[:, own : 2 * own].astype(BF16)
    values = (mixed[:, 2 * own :] + value_bias.astype(F32)).astype(BF16)
    packed = swap_ctx(
        jnp.concatenate([to_query_units(query), to_key_units(keys), to_key_units(values)], axis=1)
    )
    sizes = (query_block, half_tok, query_tile, key_tile)
    flops = 4 * query_count * length * LANES
    context_units, attended, logs = call_local(
        functools.partial(forward_kernel, *sizes),
        [
            jax.ShapeDtypeStruct((ctx, 2 * query_block, LANES), BF16),
            jax.ShapeDtypeStruct((LANES, query_count), F32),
            jax.ShapeDtypeStruct((2, query_count), F32),
        ],
        [
            pltpu.VMEM((query_count, LANES), BF16),
            pltpu.VMEM((length, LANES), BF16),
            pltpu.VMEM((length, LANES), BF16),
            pltpu.VMEM((LANES, length), BF16),
        ],
        flops,
        order, counts, slopes, packed, query_row, key_column,
    )
    context = from_query_units(swap_ctx(context_units))
    projected = scatter(jnp.dot(context, dense_weight, preferred_element_type=F32).astype(BF16))
    middle = inputs + projected.astype(F32) + dense_shift
    normed_two, scaled_second, inverse_second = norm_forward(middle, gain_second, shift_second)
    normed_two_all = gather(normed_two.astype(BF16))
    hidden = jnp.dot(normed_two_all, up_own, preferred_element_type=F32) + up_bias.astype(F32)
    activated, gelu_back = jax.vjp(gelu_tanh, hidden)
    active = activated.astype(BF16)
    branch = scatter(jnp.dot(active, down_weight, preferred_element_type=F32).astype(BF16))
    layer_out = (middle + branch.astype(F32) + down_shift).astype(BF16)[None]

    grad_active = dot(grad_all, down_weight, ((1,), (1,)))
    grad_hidden = gelu_back(grad_active)[0].astype(BF16)
    grad_normed_two = scatter(dot(grad_hidden, up_own, ((1,), (1,))).astype(BF16)).astype(F32)
    grad_middle_part, grad_gain_second, grad_shift_second = norm_backward(
        grad_normed_two, scaled_second, inverse_second, gain_second
    )
    grad_middle = cotangent[0].astype(F32) + grad_middle_part
    grad_proj_all = gather(grad_middle.astype(BF16))
    grad_context = dot(grad_proj_all, dense_weight, ((1,), (1,))).astype(BF16)
    grad_units = swap_ctx(to_query_units(grad_context))
    (grad_packed,) = call_local(
        functools.partial(backward_kernel, *sizes),
        [jax.ShapeDtypeStruct(packed.shape, BF16)],
        [
            pltpu.VMEM((query_count, LANES), BF16),
            pltpu.VMEM((length, LANES), BF16),
            pltpu.VMEM((length, LANES), BF16),
            pltpu.VMEM((LANES, length), BF16),
            pltpu.VMEM((query_count, LANES), BF16),
            pltpu.VMEM((length, LANES), F32),
            pltpu.VMEM((length, LANES), F32),
        ],
        flops * 5 // 2,
        order, counts, slopes, packed, query_row, key_column, attended, logs, grad_units,
    )
    grad_packed = swap_ctx(grad_packed)
    first_key = 2 * query_block
    first_value = first_key + count_tok
    grad_query = from_query_units(grad_packed[:, :first_key])
    grad_keys = from_key_units(grad_packed[:, first_key:first_value])
    grad_values = from_key_units(grad_packed[:, first_value:])
    grad_mixed = jnp.concatenate([grad_query, grad_keys, grad_values], axis=1)
    grad_normed = scatter(dot(grad_mixed, qkv_own, ((1,), (1,))).astype(BF16)).astype(F32)
    grad_input_part, grad_gain_first, grad_shift_first = norm_backward(
        grad_normed, scaled_first, inverse_first, gain_first
    )
    input_grad = (grad_middle + grad_input_part).astype(BF16)[None]

    def sum_rows(value):
        part = lax.psum_scatter(value.astype(BF16), "ctx", scatter_dimension=0, tiled=True)
        return lax.all_gather(part, "ctx", axis=0, tiled=True).astype(F32)

    def sum_turned(value, groups):
        rows = own // ctx
        part = lax.psum_scatter(
            value.astype(BF16).reshape(wsh, ctx, rows, value.shape[1]),
            "ctx", scatter_dimension=1, tiled=True,
        ).reshape(wsh, rows, value.shape[1])
        part = lax.all_to_all(part, "wsh", split_axis=0, concat_axis=0, tiled=True)
        part = lax.all_gather(part, "ctx", axis=0, tiled=False)
        each = value.shape[1] // groups
        full = part.astype(F32).reshape(ctx, wsh, rows, groups, each)
        return full.transpose(0, 2, 3, 1, 4).reshape(own, wsh * value.shape[1])

    grad_down_weight = sum_rows(dot(active, grad_all, ((0,), (0,))))
    grad_up_weight = sum_turned(dot(normed_two_all, grad_hidden, ((0,), (0,))), 1)
    grad_dense_weight = sum_rows(dot(context, grad_proj_all, ((0,), (0,))))
    grad_qkv_weight = sum_turned(dot(normed_all, grad_mixed, ((0,), (0,))), 3)
    norms = jnp.stack([grad_gain_first, grad_shift_first, grad_gain_second, grad_shift_second])
    norms = lax.psum_scatter(norms, "wsh", scatter_dimension=1, tiled=True)
    start = lax.axis_index("wsh") * own
    vectors_own = jnp.concatenate(
        [
            norms.reshape(-1),
            column_sum(grad_query),
            column_sum(grad_values),
            column_sum(lax.dynamic_slice_in_dim(grad_proj_all, start, own, 1)),
            column_sum(lax.dynamic_slice_in_dim(grad_all, start, own, 1)),
            column_sum(grad_hidden),
        ]
    )
    sums = lax.psum(vectors_own, "ctx")
    (
        sum_gain_first, sum_shift_first, sum_gain_second, sum_shift_second,
        sum_query, sum_value, sum_dense, sum_down,
    ) = sums[: 8 * own].reshape(8, own)
    return (
        layer_out, input_grad, sum_gain_first, sum_shift_first, grad_qkv_weight, sum_query,
        sum_value, grad_dense_weight, sum_dense, sum_gain_second, sum_shift_second,
        grad_up_weight, sums[8 * own :], grad_down_weight, sum_down,
    )


def solution(mesh):
    rows, vec, tok = P("wsh", None), P("wsh"), P("wsh", "ctx", None)
    in_specs = (
        tok, P(), rows, vec, vec, rows, vec, vec, rows, vec, vec, vec, rows, vec, rows, vec, tok,
    )
    out_specs = (
        tok, tok, vec, vec, rows, vec, vec, rows, vec, vec, vec, rows, vec, rows, vec,
    )
    return jax.shard_map(body, mesh=mesh, in_specs=in_specs, out_specs=out_specs, check_vma=False)
```

time: 1320 us -> 947 us (0.72)
  local copies, waits for them, and re-layouts: 274 us -> 67.7 us
  waiting for transfers between devices: 694 us -> 580 us
  matrix products: 134 us -> 55 us
  other arithmetic: 87.4 us -> 32.8 us
  Pallas kernels: 0 us -> 49.7 us
  starting transfers between devices: 0.52 us -> 29.5 us
  blocking collectives: 81.3 us -> 107 us
  loops' own time: 23 us -> 0 us
    psum x1 -> x0, waiting for transfers between devices: 156 us -> none  [body(): lax.psum(for_sending(tuple(owned)), 'ctx')]
    all_to_all x0 -> x6, waiting for transfers between devices: none -> 137 us  [the longest x3 72.8 us: swap_ctx(): return lax.all_to_all(value, 'ctx', split_axis=0, concat_axis=0, tiled=True)]
    reduce_scatter x6 -> x7, waiting for transfers between devices: 403 us -> 303 us  [the longest x2 121 us: sum_rows(): lax.psum_scatter(value.astype(BF16), 'ctx', scatter_dimension=0, tiled=True)]
    gather x17 -> x0, local copies, waits for them, and re-layouts: 91.5 us -> none  [the longest x16 89.8 us: pick_rows(): picked = jnp.take(table, order_ids, axis=0)]
    dot_general x47 -> x12, matrix products: 134 us -> 55 us  [the longest x8 36.2 us: dot(): return lax.dot_general(a, b, (dims, ((), ())), preferred_element_type=F32)]
    reshape x28 -> x18, local copies, waits for them, and re-layouts: 85.6 us -> 31.5 us  [the longest x4 19.5 us: sum_turned(): return full.transpose(0, 2, 3, 1, 4).reshape(own, wsh * value.shape[1])]
    pallas_call x0 -> x2, Pallas kernels: none -> 49.7 us  [call_local(): pl.pallas_call(kernel, out_shape=outs, in_specs=[smem] * 3 + [vmem] * (le...]
    select_n x13 -> x0, other arithmetic: 32.4 us -> none  [the longest x8 32.4 us: pick_rows(): picked = jnp.take(table, order_ids, axis=0)]
  transfers between devices with their start and end apart: 13 -> 22, of which waited for: 10 -> 17; matrix products, arithmetic and copies ran while one was open for 17% -> 9% of each run, Pallas kernels for 0% -> 3%
where the time goes in v1:
time: 947 us; the launch traced here: 937 us
  waiting for transfers between devices  580 us (61%)
  blocking collectives  107 us (11%)
  local copies, waits for them, and re-layouts  67.7 us (7%)
  matrix products  55 us (6%)
  Pallas kernels  49.7 us (5%)
  other arithmetic  32.8 us (3%)
  starting transfers between devices  29.5 us (3%)
  between operations  14.9 us (2%)
    reduce_scatter x2, waiting for transfers between devices, sum_rows(): lax.psum_scatter(value.astype(BF16), 'ctx', scatter_dimension=0, tiled=True)  121 us
    reduce_scatter x4, waiting for transfers between devices, scatter(): return lax.psum_scatter(value, 'wsh', scatter_dimension=0, tiled=True)  118 us
    all_to_all x3, waiting for transfers between devices, swap_ctx(): return lax.all_to_all(value, 'ctx', split_axis=0, concat_axis=0, tiled=True)  72.8 us
    reduce_scatter x1, waiting for transfers between devices, sum_turned(): lax.psum_scatter(value.astype(BF16).reshape(wsh, ctx, rows, value.shape[1...  64.2 us
    pallas_call x2, Pallas kernels, call_local(): pl.pallas_call(kernel, out_shape=outs, in_specs=[smem] * 3 + [vmem] * (le...  49.7 us
    all_gather x2, waiting for transfers between devices, sum_turned(): part = lax.all_gather(part, 'ctx', axis=0, tiled=False)  46.9 us
    all_gather x1, waiting for transfers between devices, sum_rows(): return lax.all_gather(part, 'ctx', axis=0, tiled=True).astype(F32)  38.4 us
    dot_general x8, matrix products, dot(): return lax.dot_general(a, b, (dims, ((), ())), preferred_element_type=F32)  36.2 us
  transfers between devices with their start and end apart: 22, of which 17 were waited for; matrix products, arithmetic and copies ran while one was open for 9% of the time, Pallas kernels for 3%

profile of v1, /device:TPU:0, one launch (start us, length us, event | category | flops | bytes accessed | tf_op | source)
XLA Modules:
  0.0 937.3 jit_solution(9873582433294586348)
XLA Ops:
  13.9 6.2 all_gather.37
  32.0 30.1 %all-to-all-done = bf16[256,3,4,256]{0,3,1,2:T(8,128)(2,1)} async-done(((bf16[256,3,4,256]{0,3,1,2:T(8,128)(2,1)}), bf16[256,3,4,256]{0,3,1,2:T(8,128)(2,1)}, u32[]{:S(2)}, u32[]{:S(2)}) %all-to-all-start) | async-done | bytes 1572896 | tf_op jit(solution)/shard_map/all_to_all | solution.py:270
  78.0 5.6 all-to-all-start.1
  91.2 29.7 %all-to-all-done.1.packed_ref = bf16[8,768,128]{2,1,0:T(8,128)(2,1)} async-done(((bf16[8,768,128]{2,1,0:T(8,128)(2,1)}), bf16[8,768,128]{2,1,0:T(8,128)(2,1)}, u32[]{:S(2)}, u32[]{:S(2)}) %all-to-all-start.1) | async-done | bytes 1572896 | tf_op jit(solution)/shard_map/all_to_all | solution.py:262
  120.9 24.8 %shard_map.280 = (bf16[8,256,128]{2,1,0:T(8,128)(2,1)S(1)}, f32[128,2048]{1,0:T(8,128)S(1)}, f32[2,2048]{1,0:T(2,128)S(1)}) custom-call(s32[16]{0:T(128)S(1)} %select_reduce_fusion.order_ref, s32[8]{0:T(128)S(1)} %convert_reduce_fusion.8.count_ref, f32[2]{0:T(128)S(1)} %multiply_power_fusion.slope_ref, bf16[8,768,128]{2,1,0:T(8,128)(2,1)} %all-to-all-done.1.packed_ref, ...), custom_call_target="tpu_custom_call" | custom-call | flops 2147483648 | bytes 6000000 | tf_op jit(solution)/shard_map/pallas_call | solution.py:222
  145.7 19.2 %all_to_all.60 = bf16[8,256,128]{2,1,0:T(8,128)(2,1)S(1)} all-to-all(bf16[8,256,128]{2,1,0:T(8,128)(2,1)S(1)} %get-tuple-element.18), channel_id=1, replica_groups=mesh['ctx'=8,'wsh'=4] {'ctx'}, dimensions={0} | all-to-all | bytes 1048576 | tf_op jit(solution)/shard_map/all_to_all | solution.py:262
  168.3 29.7 %reduce-scatter.14.cloned.1.call-done = bf16[256,1024]{1,0:T(8,128)(2,1)} async-done(((bf16[1024,1024]{1,0:T(8,128)(2,1)}), bf16[256,1024]{1,0:T(8,128)(2,1)}) %reduce-scatter.14.cloned.1.call-update) | async-done | bytes 524304 | tf_op jit(solution)/shard_map/reduce_scatter | solution.py:259
  212.1 34.5 %all-to-all-done.3 = bf16[256,4,1024]{0,2,1:T(8,128)(2,1)} async-done(((bf16[256,4,1024]{0,2,1:T(8,128)(2,1)}), bf16[256,4,1024]{0,2,1:T(8,128)(2,1)}, u32[]{:S(2)}, u32[]{:S(2)}) %all-to-all-start.3) | async-done | bytes 2097184 | tf_op jit(solution)/shard_map/all_to_all | solution.py:274
  250.5 6.6 fusion.58
  258.8 7.5 convert_reduce_fusion
  271.4 6.3 convolution_convert_fusion.2
  277.8 25.1 %reduce-scatter.18.cloned.1.call-done = bf16[256,1024]{1,0:T(8,128)(2,1)} async-done(((bf16[1024,1024]{1,0:T(8,128)(2,1)}), bf16[256,1024]{1,0:T(8,128)(2,1)}) %reduce-scatter.18.cloned.1.call-update) | async-done | bytes 524304 | tf_op jit(solution)/shard_map/reduce_scatter | solution.py:259
  304.6 32.7 %reduce-scatter.16.cloned.1.call-done = bf16[256,1024]{1,0:T(8,128)(2,1)} async-done(((bf16[1024,1024]{1,0:T(8,128)(2,1)}), bf16[256,1024]{1,0:T(8,128)(2,1)}) %reduce-scatter.16.cloned.1.call-update) | async-done | bytes 524304 | tf_op jit(solution)/shard_map/reduce_scatter | solution.py:259
  340.6 22.8 %all-gather.16.cloned.1.call-done = bf16[1024,1024]{1,0:T(8,128)(2,1)} async-done(((bf16[256,1024]{1,0:T(8,128)(2,1)}), bf16[1024,1024]{1,0:T(8,128)(2,1)}) %all-gather.16.cloned.1.call-update) | async-done | bytes 2097168 | tf_op jit(solution)/shard_map/all_gather | solution.py:256
  372.5 5.9 convolution_convert_fusion
  378.4 8.8 all-to-all-done.4.grad_ref
  387.2 25.0 %shard_map.281 = bf16[8,768,128]{2,1,0:T(8,128)(2,1)} custom-call(s32[16]{0:T(128)S(1)} %select_reduce_fusion.order_ref, s32[8]{0:T(128)S(1)} %convert_reduce_fusion.8.count_ref, f32[2]{0:T(128)S(1)} %multiply_power_fusion.slope_ref, bf16[8,768,128]{2,1,0:T(8,128)(2,1)} %all-to-all-done.1.packed_ref, f32[1,2048]{1,0:T(1,128)S(1)} %get-tuple-element.53.query_pos_ref, ...), custom_call_target="tpu_custom_call" | custom-call | flops 5368709120 | bytes 6000000 | tf_op jit(solution)/shard_map/pallas_call | solution.py:222
  416.6 7.2 fusion.13
  423.9 34.3 %all-to-all-done.5 = bf16[8,768,128]{2,1,0:T(8,128)(2,1)S(1)} async-done(((bf16[8,768,128]{2,1,0:T(8,128)(2,1)}), bf16[8,768,128]{2,1,0:T(8,128)(2,1)S(1)}, u32[]{:S(2)}, u32[]{:S(2)}) %all-to-all-start.5) | async-done | bytes 1572896 | tf_op jit(solution)/shard_map/all_to_all | solution.py:262
  470.7 29.7 %all-reduce.3.cloned.1.call-done = bf16[4,8,32,1024]{3,2,1,0:T(8,128)(2,1)} async-done(((bf16[4,8,32,1024]{3,2,1,0:T(8,128)(2,1)}), bf16[4,8,32,1024]{3,2,1,0:T(8,128)(2,1)}) %all-reduce.3.cloned.1.call-update) | async-done | bytes 2097168
  502.1 9.1 all_to_all.61
  511.3 60.6 %reduce-scatter.26.cloned.1.call-done = bf16[128,1024]{1,0:T(8,128)(2,1)} async-done(((bf16[1024,1024]{1,0:T(8,128)(2,1)}), bf16[128,1024]{1,0:T(8,128)(2,1)}) %reduce-scatter.26.cloned.1.call-update) | async-done | bytes 262160 | tf_op jit(solution)/shard_map/reduce_scatter | solution.py:395
  575.3 64.2 %reduce-scatter.22.cloned.1.call-done = bf16[4,1,32,768]{3,2,0,1:T(8,128)(2,1)} async-done(((bf16[4,8,32,768]{3,2,0,1:T(8,128)(2,1)}), bf16[4,1,32,768]{3,2,0,1:T(8,128)(2,1)}) %reduce-scatter.22.cloned.1.call-update) | async-done | bytes 196624 | tf_op jit(solution)/shard_map/reduce_scatter | solution.py:400
  642.9 30.1 %reduce-scatter.20.cloned.1.call-done = bf16[256,1024]{1,0:T(8,128)(2,1)} async-done(((bf16[1024,1024]{1,0:T(8,128)(2,1)}), bf16[256,1024]{1,0:T(8,128)(2,1)}) %reduce-scatter.20.cloned.1.call-update) | async-done | bytes 524304 | tf_op jit(solution)/shard_map/reduce_scatter | solution.py:259
  677.6 46.9 %all-gather.24.cloned.1.call-done = bf16[32,32,1024]{2,1,0:T(8,128)(2,1)} async-done(((bf16[4,32,1024]{2,1,0:T(8,128)(2,1)}), bf16[32,32,1024]{2,1,0:T(8,128)(2,1)}) %all-gather.24.cloned.1.call-update) | async-done | bytes 2097168 | tf_op jit(solution)/shard_map/all_gather | solution.py:405
  729.3 5.8 copy.135
  736.3 38.4 %all-gather.18.cloned.1.call-done = bf16[1024,1024]{1,0:T(8,128)(2,1)} async-done(((bf16[128,1024]{1,0:T(8,128)(2,1)}), bf16[1024,1024]{1,0:T(8,128)(2,1)}) %all-gather.18.cloned.1.call-update) | async-done | bytes 2097168 | tf_op jit(solution)/shard_map/all_gather | solution.py:396
  778.7 60.5 %reduce-scatter.24.cloned.1.call-done = bf16[32,1024]{1,0:T(8,128)(2,1)} async-done(((bf16[256,1024]{1,0:T(8,128)(2,1)}), bf16[32,1024]{1,0:T(8,128)(2,1)}) %reduce-scatter.24.cloned.1.call-update) | async-done | bytes 65552 | tf_op jit(solution)/shard_map/reduce_scatter | solution.py:395
  839.2 31.9 %all_gather.44 = bf16[256,1024]{1,0:T(8,128)(2,1)S(1)} all-gather(bf16[32,1024]{1,0:T(8,128)(2,1)} %reduce-scatter.24.cloned.1.call-done), channel_id=1, replica_groups=mesh['ctx'=8,'wsh'=4] {'ctx'}, dimensions={0}, use_global_device_ids=true | all-gather | bytes 589824 | tf_op jit(solution)/shard_map/all_gather | solution.py:396
  876.7 35.7 %psum.7 = f32[3072]{0:T(1024)S(1)} all-reduce(f32[3072]{0:T(1024)S(1)} %constant_dynamic-update-slice_fusion.1), channel_id=1, replica_groups=mesh['ctx'=8,'wsh'=4] {'ctx'}, use_global_device_ids=true, to_apply=%region_24.25 | all-reduce | flops 3072 | bytes 24576 | tf_op jit(solution)/shard_map/psum | solution.py:427
  913.5 5.6 reshape.238
  919.1 6.0 copy.123
  (197 shorter events, 136.0 us)
Async XLA Ops:
  7.2 251.6 %copy-start = (bf16[1024,1024]{1,0:T(8,128)(2,1)S(1)}, bf16[1024,1024]{1,0:T(8,128)(2,1)}, u32[]{:S(2)}) copy-start(bf16[1024,1024]{1,0:T(8,128)(2,1)} %param.31) | copy-start | bytes 6291460
  7.2 59.0 %all-gather.12.cloned.1.call-start = ((), (), s32[]{:S(2)}) async-start(), calls=%async_computation.16 | async-start | bytes 2621440 | tf_op jit(solution)/shard_map/all_gather | solution.py:256
  27.5 34.6 %all-to-all-start = ((bf16[256,3,4,256]{0,3,1,2:T(8,128)(2,1)}), bf16[256,3,4,256]{0,3,1,2:T(8,128)(2,1)}, u32[]{:S(2)}, u32[]{:S(2)}) async-start(bf16[256,3,4,256]{0,3,1,2:T(8,128)(2,1)} %copy.108), calls=%async_computation | async-start | bytes 3145728 | tf_op jit(solution)/shard_map/all_to_all | solution.py:270
  78.0 42.8 %all-to-all-start.1 = ((bf16[8,768,128]{2,1,0:T(8,128)(2,1)}), bf16[8,768,128]{2,1,0:T(8,128)(2,1)}, u32[]{:S(2)}, u32[]{:S(2)}) async-start(bf16[8,768,128]{2,1,0:T(8,128)(2,1)} %pad_maximum_fusion), calls=%async_computation.1 | async-start | bytes 3145728 | tf_op jit(solution)/shard_map/all_to_all | solution.py:262
  83.7 114.4 %reduce-scatter.14.cloned.1.call-start = ((), (), s32[]{:S(2)}) async-start(), calls=%async_computation.17 | async-start | bytes 2621440 | tf_op jit(solution)/shard_map/reduce_scatter | solution.py:259
  145.6 19.2 %copy-start.2 = (f32[128,2048]{1,0:T(8,128)}, f32[128,2048]{1,0:T(8,128)S(1)}, u32[]{:S(2)}) copy-start(f32[128,2048]{1,0:T(8,128)S(1)} %get-tuple-element.19.attended_ref) | copy-start | bytes 3145732
  145.6 20.6 %copy-start.17 = (bf16[256,1024]{1,0:T(8,128)(2,1)S(1)}, bf16[256,1024]{1,0:T(8,128)(2,1)}, u32[]{:S(2)}) copy-start(bf16[256,1024]{1,0:T(8,128)(2,1)} %param.25) | copy-start | bytes 1572868
  168.3 82.3 %all-gather.14.cloned.1.call-start = ((), (), s32[]{:S(2)}) async-start(), calls=%async_computation.18 | async-start | bytes 2621440 | tf_op jit(solution)/shard_map/all_gather | solution.py:256
  202.3 56.5 %all-gather.20.cloned.1.call-start = ((), (), s32[]{:S(2)}) async-start(), calls=%async_computation.27 | async-start | bytes 2621440 | tf_op jit(solution)/shard_map/all_gather | solution.py:256
  206.9 39.7 %all-to-all-start.3 = ((bf16[256,4,1024]{0,2,1:T(8,128)(2,1)}), bf16[256,4,1024]{0,2,1:T(8,128)(2,1)}, u32[]{:S(2)}, u32[]{:S(2)}) async-start(bf16[256,4,1024]{0,2,1:T(8,128)(2,1)} %bitcast.196), calls=%async_computation.4 | async-start | bytes 4194304 | tf_op jit(solution)/shard_map/all_to_all | solution.py:274
  211.6 91.3 %reduce-scatter.18.cloned.1.call-start = ((), (), s32[]{:S(2)}) async-start(), calls=%async_computation.20 | async-start | bytes 2621440 | tf_op jit(solution)/shard_map/reduce_scatter | solution.py:259
  271.3 66.0 %reduce-scatter.16.cloned.1.call-start = ((), (), s32[]{:S(2)}) async-start(), calls=%async_computation.19 | async-start | bytes 2621440 | tf_op jit(solution)/shard_map/reduce_scatter | solution.py:259
  277.7 25.2 %copy-start.5 = (bf16[1,256,1024]{2,1,0:T(8,128)(2,1)S(1)}, bf16[1,256,1024]{2,1,0:T(8,128)(2,1)}, u32[]{:S(2)}) copy-start(bf16[1,256,1024]{2,1,0:T(8,128)(2,1)} %param.17) | copy-start | bytes 1572868
  277.7 25.2 %copy-start.7 = (bf16[256,1024]{1,0:T(8,128)(2,1)S(1)}, bf16[256,1024]{1,0:T(8,128)(2,1)}, u32[]{:S(2)}) copy-start(bf16[256,1024]{1,0:T(8,128)(2,1)} %reduce-scatter.14.cloned.1.call-done) | copy-start | bytes 1572868
  277.7 59.6 %copy-start.11 = (bf16[1,256,1024]{2,1,0:T(8,128)(2,1)S(1)}, bf16[1,256,1024]{2,1,0:T(8,128)(2,1)}, u32[]{:S(2)}) copy-start(bf16[1,256,1024]{2,1,0:T(8,128)(2,1)} %param.33) | copy-start | bytes 1572868
  277.7 85.7 %all-gather.16.cloned.1.call-start = ((), (), s32[]{:S(2)}) async-start(), calls=%async_computation.21 | async-start | bytes 2621440 | tf_op jit(solution)/shard_map/all_gather | solution.py:256
  337.3 26.1 %copy-start.18 = (bf16[256,1024]{1,0:T(8,128)(2,1)S(1)}, bf16[256,1024]{1,0:T(8,128)(2,1)}, u32[]{:S(2)}) copy-start(bf16[256,1024]{1,0:T(8,128)(2,1)} %param.25) | copy-start | bytes 1572868
  366.7 20.5 %all-to-all-start.4 = ((bf16[8,256,128]{2,1,0:T(8,128)(2,1)}), bf16[8,256,128]{2,1,0:T(8,128)(2,1)S(1)}, u32[]{:S(2)}, u32[]{:S(2)}) async-start(bf16[8,256,128]{2,1,0:T(8,128)(2,1)} %bitcast.29), calls=%async_computation.7 | async-start | bytes 1048576 | tf_op jit(solution)/shard_map/all_to_all | solution.py:262
  372.2 128.2 %all-reduce.3.cloned.1.call-start = ((), (), s32[]{:S(2)}) async-start(), calls=%async_computation.31 | async-start | bytes 4194304
  412.2 46.1 %all-to-all-start.5 = ((bf16[8,768,128]{2,1,0:T(8,128)(2,1)}), bf16[8,768,128]{2,1,0:T(8,128)(2,1)S(1)}, u32[]{:S(2)}, u32[]{:S(2)}) async-start(bf16[8,768,128]{2,1,0:T(8,128)(2,1)} %shard_map.281), calls=%async_computation.8 | async-start | bytes 3145728 | tf_op jit(solution)/shard_map/all_to_all | solution.py:262
  416.6 155.3 %reduce-scatter.26.cloned.1.call-start = ((), (), s32[]{:S(2)}) async-start(), calls=%async_computation.25 | async-start | bytes 2359296 | tf_op jit(solution)/shard_map/reduce_scatter | solution.py:395
  423.9 215.6 %reduce-scatter.22.cloned.1.call-start = ((), (), s32[]{:S(2)}) async-start(), calls=%async_computation.23 | async-start | bytes 1769472 | tf_op jit(solution)/shard_map/reduce_scatter | solution.py:400
  464.4 208.6 %reduce-scatter.20.cloned.1.call-start = ((), (), s32[]{:S(2)}) async-start(), calls=%async_computation.22 | async-start | bytes 2621440 | tf_op jit(solution)/shard_map/reduce_scatter | solution.py:259
  469.5 102.7 %copy-start.9 = (bf16[4,2,1,2,128,128]{5,1,4,3,0,2:T(2,128)(2,1)S(1)}, bf16[4,2,1,2,128,128]{5,1,4,3,0,2:T(2,128)(2,1)}, u32[]{:S(2)}) copy-start(bf16[4,2,1,2,128,128]{5,1,4,3,0,2:T(2,128)(2,1)} %copy-done.8) | copy-start | bytes 1572868
  469.5 255.0 %all-gather.24.cloned.1.call-start = ((), (), s32[]{:S(2)}) async-start(), calls=%async_computation.29 | async-start | bytes 2359296 | tf_op jit(solution)/shard_map/all_gather | solution.py:405
  511.2 263.4 %all-gather.18.cloned.1.call-start = ((), (), s32[]{:S(2)}) async-start(), calls=%async_computation.26 | async-start | bytes 2359296 | tf_op jit(solution)/shard_map/all_gather | solution.py:396
  571.9 267.3 %reduce-scatter.24.cloned.1.call-start = ((), (), s32[]{:S(2)}) async-start(), calls=%async_computation.24 | async-start | bytes 589824 | tf_op jit(solution)/shard_map/reduce_scatter | solution.py:395
  639.5 37.4 %all-to-all-start.6 = ((bf16[4,32,768]{2,1,0:T(8,128)(2,1)}), bf16[4,32,768]{2,1,0:T(8,128)(2,1)S(1)}, u32[]{:S(2)}, u32[]{:S(2)}) async-start(bf16[4,32,768]{2,1,0:T(8,128)(2,1)} %bitcast.222), calls=%async_computation.11 | async-start | bytes 393216 | tf_op jit(solution)/shard_map/all_to_all | solution.py:404
  642.9 232.8 %reduce-scatter.28.cloned.1.call-start = ((), (), s32[]{:S(2)}) async-start(), calls=%async_computation.30 | async-start | bytes 655360
  675.7 237.9 %all-gather.22.cloned.1.call-start = ((), (), s32[]{:S(2)}) async-start(), calls=%async_computation.28 | async-start | bytes 1769472 | tf_op jit(solution)/shard_map/all_gather | solution.py:405
  778.7 95.7 %copy-start.10 = (f32[256,1024]{1,0:T(8,128)S(1)}, f32[256,1024]{1,0:T(8,128)}, u32[]{:S(2)}) copy-start(f32[256,1024]{1,0:T(8,128)} %get-tuple-element.30) | copy-start | bytes 3145732
  778.7 95.7 %copy-start.12 = (bf16[256,1024]{1,0:T(8,128)(2,1)S(1)}, bf16[256,1024]{1,0:T(8,128)(2,1)}, u32[]{:S(2)}) copy-start(bf16[256,1024]{1,0:T(8,128)(2,1)} %reduce-scatter.20.cloned.1.call-done) | copy-start | bytes 1572868
  (18 other events, 71.1 us)
Sparse Core Ops, SparseCore 0:
  22.4 34.3 all-gather.11
  168.4 29.6 reduce-scatter.13
  202.4 31.4 all-gather.13
  235.4 23.3 all-gather.19
  271.4 31.4 reduce-scatter.17
  305.9 31.4 reduce-scatter.15
  340.7 22.6 all-gather.15
  378.5 121.8 all-reduce.2
  504.4 67.4 reduce-scatter.25
  575.5 63.9 reduce-scatter.21
  642.6 30.3 reduce-scatter.19
  675.2 49.2 all-gather.23
  726.8 47.7 all-gather.17
  778.8 60.3 reduce-scatter.23
  842.1 20.6 reduce-scatter.27
  865.1 44.0 all-gather.21

commit v2 on v1

--- a/solution.py
+++ b/solution.py
@@ -228,6 +228,139 @@
         cost_estimate=pl.CostEstimate(flops=flops, bytes_accessed=6_000_000, transcendentals=flops // 256),
         compiler_params=pltpu.CompilerParams(vmem_limit_bytes=48 * 1024 * 1024),
     )(*args)
+
+
+def add_low(a, b):
+    return (a.astype(F32) + b.astype(F32)).astype(BF16)
+
+
+def ring_place(index, count):
+    odd = index % 2
+    return (1 - odd) * (index // 2) + odd * (count - 1 - index // 2)
+
+
+def ring_index(place, count):
+    late = place // (count // 2)
+    return (1 - late) * 2 * place + late * (2 * (count - 1 - place) + 1)
+
+
+def sum_kernel(
+    count, peers, turned, part_ref, out_ref, held, mine,
+    send_sem, recv_sem, turn_send, turn_recv, back_send, back_recv,
+):
+    place = ring_place(lax.axis_index("ctx"), count)
+    me = lax.axis_index("wsh")
+    sides = (
+        ring_index((place + 1) % count, count), ring_index((place + count - 1) % count, count)
+    )
+    barrier = pltpu.get_barrier_semaphore()
+    for side in sides:
+        pl.semaphore_signal(
+            barrier, inc=1, device_id={"ctx": side}, device_id_type=pl.DeviceIdType.MESH
+        )
+    for step in range(1, peers):
+        pl.semaphore_signal(
+            barrier, inc=1, device_id={"wsh": (me + step) % peers},
+            device_id_type=pl.DeviceIdType.MESH,
+        )
+    pl.semaphore_wait(barrier, 1 + peers)
+
+    def chunk(way, back):
+        return (place + count - back) % count if way == 0 else (place + back) % count
+
+    def send(way, step, src):
+        return pltpu.make_async_remote_copy(
+            src_ref=src, dst_ref=held.at[step, way],
+            send_sem=send_sem.at[step, way], recv_sem=recv_sem.at[step, way],
+            device_id={"ctx": sides[way]}, device_id_type=pl.DeviceIdType.MESH,
+        )
+
+    for way in range(2):
+        send(way, 0, part_ref.at[chunk(way, 1), way]).start()
+
+    def reduce_step(step, _):
+        for way in range(2):
+            here = held.at[step - 1, way]
+            send(way, step - 1, here).wait_recv()
+            here[...] = add_low(here[...], part_ref[chunk(way, step + 1), way])
+            send(way, step, here).start()
+        return 0
+
+    lax.fori_loop(1, count - 1, reduce_step, 0)
+    for way in range(2):
+        last = held.at[count - 2, way]
+        send(way, count - 2, last).wait_recv()
+        mine[way] = add_low(last[...], part_ref[place, way])
+
+    def turn(step):
+        peer = (me + step) % peers
+        return pltpu.make_async_remote_copy(
+            src_ref=mine.at[:, pl.ds(pl.multiple_of(peer * turned, 16), turned), :],
+            dst_ref=out_ref.at[place, :, pl.ds(pl.multiple_of(me * turned, 16), turned), :],
+            send_sem=turn_send.at[step - 1], recv_sem=turn_recv.at[step - 1],
+            device_id={"wsh": peer}, device_id_type=pl.DeviceIdType.MESH,
+        )
+
+    for step in range(1, peers):
+        turn(step).start()
+    kept = pl.ds(pl.multiple_of(me * turned, 16), turned)
+    out_ref[place, :, kept, :] = mine[:, kept, :]
+    out_ref[place, :, peers * turned :, :] = mine[:, peers * turned :, :]
+    for step in range(1, peers):
+        turn(step).wait_recv()
+
+    def pass_on(way, step):
+        here = out_ref.at[chunk(way, step), way]
+        return pltpu.make_async_remote_copy(
+            src_ref=here, dst_ref=here,
+            send_sem=back_send.at[step, way], recv_sem=back_recv.at[step, way],
+            device_id={"ctx": sides[way]}, device_id_type=pl.DeviceIdType.MESH,
+        )
+
+    for way in range(2):
+        pass_on(way, 0).start()
+
+    def gather_step(step, _):
+        for way in range(2):
+            pass_on(way, step - 1).wait_recv()
+            pass_on(way, step).start()
+        return 0
+
+    lax.fori_loop(1, count - 1, gather_step, 0)
+    for way in range(2):
+        pass_on(way, count - 2).wait_recv()
+    for step in range(1, peers):
+        turn(step).wait_send()
+
+    def drain(step, _):
+        for way in range(2):
+            send(way, step, held.at[step, way]).wait_send()
+            pass_on(way, step).wait_send()
+        return 0
+
+    lax.fori_loop(0, count - 1, drain, 0)
+
+
+def sum_over_ctx(parts, turned):
+    count, _, rows, width = parts.shape
+    peers = lax.axis_size("wsh")
+    sems = pltpu.SemaphoreType.DMA((count - 1, 2))
+    turn_sems = pltpu.SemaphoreType.DMA((peers - 1,))
+    return pl.pallas_call(
+        functools.partial(sum_kernel, count, peers, turned),
+        out_shape=jax.ShapeDtypeStruct(parts.shape, BF16),
+        in_specs=[pl.BlockSpec(memory_space=pltpu.VMEM)],
+        out_specs=pl.BlockSpec(memory_space=pltpu.VMEM),
+        scratch_shapes=[
+            pltpu.VMEM((count - 1, 2, rows, width), BF16),
+            pltpu.VMEM((2, rows, width), BF16),
+            sems, sems, turn_sems, turn_sems, sems, sems,
+        ],
+        cost_estimate=pl.CostEstimate(flops=parts.size, bytes_accessed=300_000_000, transcendentals=0),
+        compiler_params=pltpu.CompilerParams(
+            collective_id=0, has_side_effects=True, vmem_limit_bytes=40 * 1024 * 1024
+        ),
+    )(parts)
 
 
 def body(
@@ -391,26 +524,35 @@
     )
     input_grad = (grad_middle + grad_input_part).astype(BF16)[None]
 
-    def sum_rows(value):
-        part = lax.psum_scatter(value.astype(BF16), "ctx", scatter_dimension=0, tiled=True)
-        return lax.all_gather(part, "ctx", axis=0, tiled=True).astype(F32)
-
-    def sum_turned(value, groups):
-        rows = own // ctx
-        part = lax.psum_scatter(
-            value.astype(BF16).reshape(wsh, ctx, rows, value.shape[1]),
-            "ctx", scatter_dimension=1, tiled=True,
-        ).reshape(wsh, rows, value.shape[1])
-        part = lax.all_to_all(part, "wsh", split_axis=0, concat_axis=0, tiled=True)
-        part = lax.all_gather(part, "ctx", axis=0, tiled=False)
-        each = value.shape[1] // groups
-        full = part.astype(F32).reshape(ctx, wsh, rows, groups, each)
-        return full.transpose(0, 2, 3, 1, 4).reshape(own, wsh * value.shape[1])
-
-    grad_down_weight = sum_rows(dot(active, grad_all, ((0,), (0,))))
-    grad_up_weight = sum_turned(dot(normed_two_all, grad_hidden, ((0,), (0,))), 1)
-    grad_dense_weight = sum_rows(dot(context, grad_proj_all, ((0,), (0,))))
-    grad_qkv_weight = sum_turned(dot(normed_all, grad_mixed, ((0,), (0,))), 3)
+    chunk = 2 * LANES
+
+    def cut(value):
+        shaped = value.astype(BF16).reshape(ctx, 2, -1, value.shape[1] // chunk, chunk)
+        return shaped.transpose(0, 1, 3, 2, 4).reshape(ctx, 2, -1, chunk)
+
+    def uncut(value, columns):
+        shaped = value.astype(F32).reshape(ctx, 2, columns // chunk, -1, chunk)
+        return shaped.transpose(0, 1, 3, 2, 4).reshape(-1, columns)
+
+    def pad_rows(value):
+        return jnp.pad(value, [(0, 0)] * (value.ndim - 2) + [(0, -value.shape[-2] % 16), (0, 0)])
+
+    turned_cols = hidden_own + 3 * own
+    groups = turned_cols // chunk
+    fine = own // (2 * ctx)
+    turned = jnp.concatenate(
+        [
+            dot(normed_two_all, grad_hidden, ((0,), (0,))).astype(BF16),
+            dot(normed_all, grad_mixed, ((0,), (0,))).astype(BF16),
+        ],
+        axis=1,
+    ).reshape(wsh, ctx, 2, fine, groups, chunk)
+    turned = pad_rows(
+        turned.transpose(1, 2, 0, 4, 3, 5).reshape(ctx, 2, wsh, groups * fine, chunk)
+    )
+    turned_rows = turned.shape[3]
+    down_part = cut(dot(active, grad_all, ((0,), (0,))))
+    dense_part = cut(dot(context, grad_proj_all, ((0,), (0,))))
     norms = jnp.stack([grad_gain_first, grad_shift_first, grad_gain_second, grad_shift_second])
     norms = lax.psum_scatter(norms, "wsh", scatter_dimension=1, tiled=True)
     start = lax.axis_index("wsh") * own
@@ -423,8 +565,31 @@
             column_sum(lax.dynamic_slice_in_dim(grad_all, start, own, 1)),
             column_sum(grad_hidden),
         ]
-    )
-    sums = lax.psum(vectors_own, "ctx")
+    ).astype(BF16)
+    piece = vectors_own.shape[0] // (2 * ctx)
+    vector_part = pad_rows(
+        jnp.pad(vectors_own.reshape(ctx, 2, 1, piece), [(0, 0)] * 3 + [(0, chunk - piece)])
+    )
+    parts = jnp.concatenate(
+        [turned.reshape(ctx, 2, -1, chunk), down_part, dense_part, vector_part], axis=2
+    )
+    summed = sum_over_ctx(parts, turned_rows)
+    at_down = wsh * turned_rows
+    at_dense = at_down + down_part.shape[2]
+    at_vector = at_dense + dense_part.shape[2]
+    back = summed[:, :, :at_down].reshape(ctx, 2, wsh, turned_rows, chunk)
+    back = back[:, :, :, : groups * fine].reshape(ctx, 2, wsh, groups, fine, chunk)
+
+    def unturn(value, sections):
+        shaped = value.astype(F32).reshape(ctx, 2, wsh, sections, -1, fine, chunk)
+        return shaped.transpose(0, 1, 5, 3, 2, 4, 6).reshape(own, -1)
+
+    up_groups = hidden_own // chunk
+    grad_up_weight = unturn(back[:, :, :, :up_groups], 1)
+    grad_qkv_weight = unturn(back[:, :, :, up_groups:], 3)
+    grad_down_weight = uncut(summed[:, :, at_down:at_dense], width)
+    grad_dense_weight = uncut(summed[:, :, at_dense:at_vector], width)
+    sums = summed[:, :, at_vector, :piece].reshape(-1).astype(F32)
     (
         sum_gain_first, sum_shift_first, sum_gain_second, sum_shift_second,
         sum_query, sum_value, sum_dense, sum_down,

time: 947 us -> 732 us (0.77)
  waiting for transfers between devices: 580 us -> 224 us
  Pallas kernels: 49.7 us -> 189 us
  local copies, waits for them, and re-layouts: 67.7 us -> 101 us
  blocking collectives: 107 us -> 92.3 us
  starting transfers between devices: 29.5 us -> 15.1 us
    reduce_scatter x3 -> x0, waiting for transfers between devices: 185 us -> none  [the longest x2 121 us: sum_rows(): lax.psum_scatter(value.astype(BF16), 'ctx', scatter_dimension=0, tiled=True)]
    pallas_call x0 -> x1, Pallas kernels: none -> 141 us  [sum_over_ctx(): pl.pallas_call(functools.partial(sum_kernel, count, peers, turned), out_s...]
    all_gather x3 -> x0, waiting for transfers between devices: 85.2 us -> none  [the longest x2 46.9 us: sum_turned(): part = lax.all_gather(part, 'ctx', axis=0, tiled=False)]
    all_to_all x1 -> x3, blocking collectives: 19.2 us -> 80.9 us  [swap_ctx(): return lax.all_to_all(value, 'ctx', split_axis=0, concat_axis=0, tiled=True)]
    all_to_all x3 -> x1, waiting for transfers between devices: 72.8 us -> 29.6 us  [swap_ctx(): return lax.all_to_all(value, 'ctx', split_axis=0, concat_axis=0, tiled=True)]
    psum x1 -> x0, blocking collectives: 35.7 us -> none  [body(): sums = lax.psum(vectors_own, 'ctx')]
    all_gather x1 -> x0, blocking collectives: 31.9 us -> none  [sum_rows(): return lax.all_gather(part, 'ctx', axis=0, tiled=True).astype(F32)]
    reduce_scatter x4, waiting for transfers between devices: 118 us -> 87.2 us  [scatter(): return lax.psum_scatter(value, 'wsh', scatter_dimension=0, tiled=True)]
  transfers between devices with their start and end apart: 22 -> 12, of which waited for: 17 -> 9; matrix products, arithmetic and copies ran while one was open for 9% -> 12% of each run, Pallas kernels for 3% -> 0%
where the time goes in v2:
time: 732 us; the launch traced here: 724 us
  waiting for transfers between devices  224 us (31%)
  Pallas kernels  189 us (26%)
  local copies, waits for them, and re-layouts  101 us (14%)
  blocking collectives  92.3 us (13%)
  matrix products  50.6 us (7%)
  other arithmetic  36.7 us (5%)
  starting transfers between devices  15.1 us (2%)
  between operations  14.9 us (2%)
    pallas_call x1, Pallas kernels, sum_over_ctx(): pl.pallas_call(functools.partial(sum_kernel, count, peers, turned), out_s...  141 us
    reduce_scatter x4, waiting for transfers between devices, scatter(): return lax.psum_scatter(value, 'wsh', scatter_dimension=0, tiled=True)  87.2 us
    all_to_all x3, blocking collectives, swap_ctx(): return lax.all_to_all(value, 'ctx', split_axis=0, concat_axis=0, tiled=True)  80.9 us
    pallas_call x2, Pallas kernels, call_local(): pl.pallas_call(kernel, out_shape=outs, in_specs=[smem] * 3 + [vmem] * (le...  48.2 us
    all_to_all x1, waiting for transfers between devices, body(): lax.all_to_all(up_weight.reshape(own, wsh, hidden_own), 'wsh', split_axis...  34.8 us
    dot_general x8, matrix products, dot(): return lax.dot_general(a, b, (dims, ((), ())), preferred_element_type=F32)  31.8 us
    all_to_all x1, waiting for transfers between devices, body(): lax.all_to_all(qkv_weight.reshape(own, 3, wsh, own), 'wsh', split_axis=2,...  30.2 us
    all_to_all x1, waiting for transfers between devices, swap_ctx(): return lax.all_to_all(value, 'ctx', split_axis=0, concat_axis=0, tiled=True)  29.6 us
  transfers between devices with their start and end apart: 12, of which 9 were waited for; matrix products, arithmetic and copies ran while one was open for 12% of the time, Pallas kernels for 0%

profile of v2, /device:TPU:0, one launch (start us, length us, event | category | flops | bytes accessed | tf_op | source)
XLA Modules:
  0.0 724.0 jit_solution(4145641263277921790)
XLA Ops:
  13.9 6.2 all_gather.19
  27.5 4.4 all-to-all-start
  32.0 30.2 %all-to-all-done = bf16[256,3,4,256]{0,3,1,2:T(8,128)(2,1)} async-done(((bf16[256,3,4,256]{0,3,1,2:T(8,128)(2,1)}), bf16[256,3,4,256]{0,3,1,2:T(8,128)(2,1)}, u32[]{:S(2)}, u32[]{:S(2)}) %all-to-all-start) | async-done | bytes 1572896 | tf_op jit(solution)/shard_map/all_to_all | solution.py:403
  78.1 5.5 all-to-all-start.1
  83.9 5.2 all-gather.1
  91.2 29.6 %all-to-all-done.1.packed_ref = bf16[8,768,128]{2,1,0:T(8,128)(2,1)} async-done(((bf16[8,768,128]{2,1,0:T(8,128)(2,1)}), bf16[8,768,128]{2,1,0:T(8,128)(2,1)}, u32[]{:S(2)}, u32[]{:S(2)}) %all-to-all-start.1) | async-done | bytes 1572896 | tf_op jit(solution)/shard_map/all_to_all | solution.py:395
  120.8 24.8 %shard_map.280 = (bf16[8,256,128]{2,1,0:T(8,128)(2,1)S(1)}, f32[128,2048]{1,0:T(8,128)S(1)}, f32[2,2048]{1,0:T(2,128)S(1)}) custom-call(s32[16]{0:T(128)S(1)} %select_reduce_fusion.order_ref, s32[8]{0:T(128)S(1)} %convert_reduce_fusion.4.count_ref, f32[2]{0:T(128)S(1)} %multiply_power_fusion.slope_ref, bf16[8,768,128]{2,1,0:T(8,128)(2,1)} %all-to-all-done.1.packed_ref, ...), custom_call_target="tpu_custom_call" | custom-call | flops 2147483648 | bytes 6000000 | tf_op jit(solution)/shard_map/pallas_call | solution.py:222
  145.6 19.1 %all_to_all.50 = bf16[8,256,128]{2,1,0:T(8,128)(2,1)S(1)} all-to-all(bf16[8,256,128]{2,1,0:T(8,128)(2,1)S(1)} %get-tuple-element.18), channel_id=1, replica_groups=mesh['ctx'=8,'wsh'=4] {'ctx'}, dimensions={0} | all-to-all | bytes 1048576 | tf_op jit(solution)/shard_map/all_to_all | solution.py:395
  168.2 29.7 %reduce-scatter.8.cloned.1.call-done = bf16[256,1024]{1,0:T(8,128)(2,1)} async-done(((bf16[1024,1024]{1,0:T(8,128)(2,1)}), bf16[256,1024]{1,0:T(8,128)(2,1)}) %reduce-scatter.8.cloned.1.call-update) | async-done | bytes 524304 | tf_op jit(solution)/shard_map/reduce_scatter | solution.py:392
  203.8 4.1 copy.145
  207.9 4.6 all-to-all-start.3
  212.8 34.8 %all-to-all-done.3 = bf16[256,4,1024]{0,2,1:T(8,128)(2,1)} async-done(((bf16[256,4,1024]{0,2,1:T(8,128)(2,1)}), bf16[256,4,1024]{0,2,1:T(8,128)(2,1)}, u32[]{:S(2)}, u32[]{:S(2)}) %all-to-all-start.3) | async-done | bytes 2097184 | tf_op jit(solution)/shard_map/all_to_all | solution.py:407
  247.6 3.9 copy.146
  251.5 6.6 fusion.61
  259.7 7.5 %fusion.59 = (bf16[1024]{0:T(1024)(128)(2,1)S(1)}, bf16[1024,1024]{1,0:T(8,128)(2,1)S(1)}) fusion(f32[1024,1024]{1,0:T(8,128)} %fusion.61, f32[1024]{0:T(1024)S(1)} %convert_element_type.166, bf16[1024,1024]{1,0:T(8,128)(2,1)S(1)} %copy-done, bf16[1,1024,1024]{2,1,0:T(8,128)(2,1)} %all-gather.13.cloned.1.call-done), kind=kOutput, calls=%fused_computation.118 | convolution fusion | flops 2170551296 | bytes 10491904 | tf_op jit(solution)/shard_map/dot_general | solution.py:42
  272.3 6.3 convolution_convert_fusion.2
  278.7 25.1 %reduce-scatter.12.cloned.1.call-done = bf16[256,1024]{1,0:T(8,128)(2,1)} async-done(((bf16[1024,1024]{1,0:T(8,128)(2,1)}), bf16[256,1024]{1,0:T(8,128)(2,1)}) %reduce-scatter.12.cloned.1.call-update) | async-done | bytes 524304 | tf_op jit(solution)/shard_map/reduce_scatter | solution.py:392
  305.9 32.4 %reduce-scatter.10.cloned.1.call-done = bf16[256,1024]{1,0:T(8,128)(2,1)} async-done(((bf16[1024,1024]{1,0:T(8,128)(2,1)}), bf16[256,1024]{1,0:T(8,128)(2,1)}) %reduce-scatter.10.cloned.1.call-update) | async-done | bytes 524304 | tf_op jit(solution)/shard_map/reduce_scatter | solution.py:392
  341.5 22.7 %all-gather.11.cloned.1.call-done = bf16[1024,1024]{1,0:T(8,128)(2,1)} async-done(((bf16[256,1024]{1,0:T(8,128)(2,1)}), bf16[1024,1024]{1,0:T(8,128)(2,1)}) %all-gather.11.cloned.1.call-update) | async-done | bytes 2097168 | tf_op jit(solution)/shard_map/all_gather | solution.py:389
  366.8 20.6 %all_to_all.51.grad_ref = bf16[8,256,128]{2,1,0:T(8,128)(2,1)S(1)} all-to-all(bf16[8,256,128]{2,1,0:T(8,128)(2,1)S(1)} %bitcast.240), channel_id=1, replica_groups=mesh['ctx'=8,'wsh'=4] {'ctx'}, dimensions={0} | all-to-all | bytes 1048576 | tf_op jit(solution)/shard_map/all_to_all | solution.py:395
  388.6 23.4 %shard_map.281 = bf16[8,768,128]{2,1,0:T(8,128)(2,1)S(1)} custom-call(s32[16]{0:T(128)S(1)} %select_reduce_fusion.order_ref, s32[8]{0:T(128)S(1)} %convert_reduce_fusion.4.count_ref, f32[2]{0:T(128)S(1)} %multiply_power_fusion.slope_ref, bf16[8,768,128]{2,1,0:T(8,128)(2,1)} %all-to-all-done.1.packed_ref, f32[1,2048]{1,0:T(1,128)S(1)} %get-tuple-element.53.query_pos_ref, ...), custom_call_target="tpu_custom_call" | custom-call | flops 5368709120 | bytes 6000000 | tf_op jit(solution)/shard_map/pallas_call | solution.py:222
  412.0 41.2 %all_to_all.52 = bf16[8,768,128]{2,1,0:T(8,128)(2,1)S(1)} all-to-all(bf16[8,768,128]{2,1,0:T(8,128)(2,1)S(1)} %shard_map.281), channel_id=1, replica_groups=mesh['ctx'=8,'wsh'=4] {'ctx'}, dimensions={0} | all-to-all | bytes 3145728 | tf_op jit(solution)/shard_map/all_to_all | solution.py:395
  459.9 6.6 fusion.15
  479.9 4.1 convolution_convert_fusion.5
  486.3 5.9 copy.152
  492.3 8.0 %reshape.265 = bf16[4,8,2,16,7,256]{5,4,3,2,1,0:T(8,128)(2,1)} reshape(bf16[1024,1792]{1,0:T(8,128)(2,1)} %copy.152) | data formatting | bytes 7340032 | tf_op jit(solution)/shard_map/reshape | solution.py:549
  500.2 5.4 copy.153
  512.8 17.7 %reduce-scatter.16.cloned.1.call-done = f32[256,4]{1,0:T(8,128)} async-done(((f32[1024,4]{1,0:T(8,128)}), f32[256,4]{1,0:T(8,128)}) %reduce-scatter.16.cloned.1.call-update) | async-done | bytes 4112
  536.1 141.2 %shard_map.282 = bf16[8,2,784,256]{3,2,1,0:T(8,128)(2,1)S(1)} custom-call(bf16[8,2,784,256]{3,2,1,0:T(8,128)(2,1)S(1)} %fusion.1.part_ref), custom_call_target="tpu_custom_call" | custom-call | flops 3211264 | bytes 300000000 | tf_op jit(solution)/shard_map/pallas_call | solution.py:349
  698.9 5.3 reshape.286
  704.3 7.0 copy.159
  711.3 5.8 reshape.290
  (190 shorter events, 114.4 us)
Async XLA Ops:
  7.2 252.5 %copy-start = (bf16[1024,1024]{1,0:T(8,128)(2,1)S(1)}, bf16[1024,1024]{1,0:T(8,128)(2,1)}, u32[]{:S(2)}) copy-start(bf16[1024,1024]{1,0:T(8,128)(2,1)} %param.31) | copy-start | bytes 6291460
  7.2 59.0 %all-gather.7.cloned.1.call-start = ((), (), s32[]{:S(2)}) async-start(), calls=%async_computation.11 | async-start | bytes 2621440 | tf_op jit(solution)/shard_map/all_gather | solution.py:389
  24.8 7.1 copy-start.25
  24.8 7.1 copy-start.26
  27.5 34.6 %all-to-all-start = ((bf16[256,3,4,256]{0,3,1,2:T(8,128)(2,1)}), bf16[256,3,4,256]{0,3,1,2:T(8,128)(2,1)}, u32[]{:S(2)}, u32[]{:S(2)}) async-start(bf16[256,3,4,256]{0,3,1,2:T(8,128)(2,1)} %copy.138), calls=%async_computation | async-start | bytes 3145728 | tf_op jit(solution)/shard_map/all_to_all | solution.py:403
  75.6 8.1 %copy-start.23 = (s32[8,2]{0,1:T(2,128)S(1)}, s32[8,2]{0,1:T(2,128)}, u32[]{:S(2)}) copy-start(s32[8,2]{0,1:T(2,128)} %param.18) | copy-start | bytes 196
  75.6 8.2 %copy-start.21 = (s32[1,2048]{1,0:T(1,128)S(1)}, s32[1,2048]{1,0:T(1,128)}, u32[]{:S(2)}) copy-start(s32[1,2048]{1,0:T(1,128)} %param.19) | copy-start | bytes 24580
  78.1 42.7 %all-to-all-start.1 = ((bf16[8,768,128]{2,1,0:T(8,128)(2,1)}), bf16[8,768,128]{2,1,0:T(8,128)(2,1)}, u32[]{:S(2)}, u32[]{:S(2)}) async-start(bf16[8,768,128]{2,1,0:T(8,128)(2,1)} %pad_maximum_fusion.1), calls=%async_computation.1 | async-start | bytes 3145728 | tf_op jit(solution)/shard_map/all_to_all | solution.py:395
  83.6 114.3 %reduce-scatter.8.cloned.1.call-start = ((), (), s32[]{:S(2)}) async-start(), calls=%async_computation.12 | async-start | bytes 2621440 | tf_op jit(solution)/shard_map/reduce_scatter | solution.py:392
  120.8 45.2 %copy-start.17 = (bf16[256,1024]{1,0:T(8,128)(2,1)S(1)}, bf16[256,1024]{1,0:T(8,128)(2,1)}, u32[]{:S(2)}) copy-start(bf16[256,1024]{1,0:T(8,128)(2,1)} %param.25) | copy-start | bytes 1572868
  145.6 19.1 %copy-start.3 = (f32[128,2048]{1,0:T(8,128)}, f32[128,2048]{1,0:T(8,128)S(1)}, u32[]{:S(2)}) copy-start(f32[128,2048]{1,0:T(8,128)S(1)} %get-tuple-element.19.attended_ref) | copy-start | bytes 3145732
  168.1 83.4 %all-gather.9.cloned.1.call-start = ((), (), s32[]{:S(2)}) async-start(), calls=%async_computation.13 | async-start | bytes 2621440 | tf_op jit(solution)/shard_map/all_gather | solution.py:389
  203.2 56.5 %all-gather.13.cloned.1.call-start = ((), (), s32[]{:S(2)}) async-start(), calls=%async_computation.18 | async-start | bytes 2621440 | tf_op jit(solution)/shard_map/all_gather | solution.py:389
  207.9 4.9 copy-start.22
  207.9 39.7 %all-to-all-start.3 = ((bf16[256,4,1024]{0,2,1:T(8,128)(2,1)}), bf16[256,4,1024]{0,2,1:T(8,128)(2,1)}, u32[]{:S(2)}, u32[]{:S(2)}) async-start(bf16[256,4,1024]{0,2,1:T(8,128)(2,1)} %bitcast.222), calls=%async_computation.4 | async-start | bytes 4194304 | tf_op jit(solution)/shard_map/all_to_all | solution.py:407
  212.5 91.3 %reduce-scatter.12.cloned.1.call-start = ((), (), s32[]{:S(2)}) async-start(), calls=%async_computation.15 | async-start | bytes 2621440 | tf_op jit(solution)/shard_map/reduce_scatter | solution.py:392
  259.7 8.8 %copy-start.15 = (bf16[4,256,1,1024]{3,1,0,2:T(8,128)(2,1)S(1)}, bf16[4,256,1,1024]{3,1,0,2:T(8,128)(2,1)}, u32[]{:S(2)}) copy-start(bf16[4,256,1,1024]{3,1,0,2:T(8,128)(2,1)} %copy.146) | copy-start | bytes 6291460
  272.3 66.0 %reduce-scatter.10.cloned.1.call-start = ((), (), s32[]{:S(2)}) async-start(), calls=%async_computation.14 | async-start | bytes 2621440 | tf_op jit(solution)/shard_map/reduce_scatter | solution.py:392
  278.6 59.6 %copy-start.5 = (bf16[1,256,1024]{2,1,0:T(8,128)(2,1)S(1)}, bf16[1,256,1024]{2,1,0:T(8,128)(2,1)}, u32[]{:S(2)}) copy-start(bf16[1,256,1024]{2,1,0:T(8,128)(2,1)} %param.17) | copy-start | bytes 1572868
  278.6 59.6 %copy-start.7 = (bf16[256,1024]{1,0:T(8,128)(2,1)S(1)}, bf16[256,1024]{1,0:T(8,128)(2,1)}, u32[]{:S(2)}) copy-start(bf16[256,1024]{1,0:T(8,128)(2,1)} %reduce-scatter.8.cloned.1.call-done) | copy-start | bytes 1572868
  278.6 59.6 %copy-start.13 = (bf16[1,256,1024]{2,1,0:T(8,128)(2,1)S(1)}, bf16[1,256,1024]{2,1,0:T(8,128)(2,1)}, u32[]{:S(2)}) copy-start(bf16[1,256,1024]{2,1,0:T(8,128)(2,1)} %param.33) | copy-start | bytes 1572868
  278.7 85.6 %copy-start.18 = (bf16[256,1024]{1,0:T(8,128)(2,1)S(1)}, bf16[256,1024]{1,0:T(8,128)(2,1)}, u32[]{:S(2)}) copy-start(bf16[256,1024]{1,0:T(8,128)(2,1)} %param.25) | copy-start | bytes 1572868
  278.7 85.5 %all-gather.11.cloned.1.call-start = ((), (), s32[]{:S(2)}) async-start(), calls=%async_computation.16 | async-start | bytes 2621440 | tf_op jit(solution)/shard_map/all_gather | solution.py:389
  341.5 166.3 %reduce-scatter.14.cloned.1.call-start = ((), (), s32[]{:S(2)}) async-start(), calls=%async_computation.17 | async-start | bytes 2621440 | tf_op jit(solution)/shard_map/reduce_scatter | solution.py:392
  459.6 70.8 %reduce-scatter.16.cloned.1.call-start = ((), (), s32[]{:S(2)}) async-start(), calls=%async_computation.19 | async-start | bytes 655360
  472.9 3.8 copy-start.9
  472.9 3.8 copy-start.11
  479.9 4.1 copy-start.12
  500.2 7.6 %copy-start.6 = (bf16[1,256,1024]{2,1,0:T(8,128)(2,1)S(1)}, bf16[1,256,1024]{2,1,0:T(8,128)(2,1)}, u32[]{:S(2)}) copy-start(bf16[1,256,1024]{2,1,0:T(8,128)(2,1)} %param.17) | copy-start | bytes 1572868
  505.6 4.9 copy-start.10
  505.6 27.1 %copy-start.14 = (bf16[8,2,16,4,256]{4,2,3,1,0:T(8,128)(2,1)S(1)}, bf16[8,2,16,4,256]{4,2,3,1,0:T(8,128)(2,1)}, u32[]{:S(2)}) copy-start(bf16[8,2,16,4,256]{4,2,3,1,0:T(8,128)(2,1)} %copy.155) | copy-start | bytes 1572868
  704.3 12.8 %copy-start.1 = (bf16[1024,1024]{1,0:T(8,128)(2,1)S(1)}, bf16[1024,1024]{1,0:T(8,128)(2,1)}, u32[]{:S(2)}) copy-start(bf16[1024,1024]{1,0:T(8,128)(2,1)} %param.31) | copy-start | bytes 6291460
  (11 other events, 23.3 us)
Sparse Core Ops, SparseCore 0:
  22.4 34.5 all-gather.6
  168.2 29.6 reduce-scatter.7
  203.4 31.3 all-gather.8
  236.3 23.3 all-gather.12
  272.4 31.4 reduce-scatter.11
  306.8 31.3 reduce-scatter.9
  341.6 22.5 all-gather.10
  459.8 29.4 reduce-scatter.13
  510.6 19.7 reduce-scatter.15

commit v3 on v2

--- a/solution.py
+++ b/solution.py
@@ -404,10 +404,6 @@
         qkv_weight.reshape(own, 3, wsh, own), "wsh", split_axis=2, concat_axis=0, tiled=True
     ).reshape(width, 3 * own)
     hidden_own = up_weight.shape[1] // wsh
-    up_own = lax.all_to_all(
-        up_weight.reshape(own, wsh, hidden_own), "wsh", split_axis=1, concat_axis=0, tiled=True
-    ).reshape(width, hidden_own)
-
     unit = lax.axis_index("ctx") // share
     part = lax.axis_index("ctx") % share
     seq_pos = lax.dynamic_index_in_dim(all_pos, unit // pairs, 0, keepdims=False)
@@ -457,6 +453,10 @@
     packed = swap_ctx(
         jnp.concatenate([to_query_units(query), to_key_units(keys), to_key_units(values)], axis=1)
     )
+    packed, up_late = lax.optimization_barrier((packed, up_weight))
+    up_own = lax.all_to_all(
+        up_late.reshape(own, wsh, hidden_own), "wsh", split_axis=1, concat_axis=0, tiled=True
+    ).reshape(width, hidden_own)
     sizes = (query_block, half_tok, query_tile, key_tile)
     flops = 4 * query_count * length * LANES
     context_units, attended, logs = call_local(
@@ -475,6 +475,7 @@
         flops,
         order, counts, slopes, packed, query_row, key_column,
     )
+    context_units, up_own = lax.optimization_barrier((context_units, up_own))
     context = from_query_units(swap_ctx(context_units))
     projected = scatter(jnp.dot(context, dense_weight, preferred_element_type=F32).astype(BF16))
     middle = inputs + projected.astype(F32) + dense_shift
@@ -483,8 +484,7 @@
     hidden = jnp.dot(normed_two_all, up_own, preferred_element_type=F32) + up_bias.astype(F32)
     activated, gelu_back = jax.vjp(gelu_tanh, hidden)
     active = activated.astype(BF16)
-    branch = scatter(jnp.dot(active, down_weight, preferred_element_type=F32).astype(BF16))
-    layer_out = (middle + branch.astype(F32) + down_shift).astype(BF16)[None]
+    branch_part = jnp.dot(active, down_weight, preferred_element_type=F32).astype(BF16)
 
     grad_active = dot(grad_all, down_weight, ((1,), (1,)))
     grad_hidden = gelu_back(grad_active)[0].astype(BF16)
@@ -494,6 +494,9 @@
     )
     grad_middle = cotangent[0].astype(F32) + grad_middle_part
     grad_proj_all = gather(grad_middle.astype(BF16))
+    branch_part, grad_proj_all = lax.optimization_barrier((branch_part, grad_proj_all))
+    branch = scatter(branch_part)
+    layer_out = (middle + branch.astype(F32) + down_shift).astype(BF16)[None]
     grad_context = dot(grad_proj_all, dense_weight, ((1,), (1,))).astype(BF16)
     grad_units = swap_ctx(to_query_units(grad_context))
     (grad_packed,) = call_local(
@@ -524,7 +527,7 @@
     )
     input_grad = (grad_middle + grad_input_part).astype(BF16)[None]
 
-    chunk = 2 * LANES
+    chunk = width
 
     def cut(value):
         shaped = value.astype(BF16).reshape(ctx, 2, -1, value.shape[1] // chunk, chunk)
@@ -537,13 +540,16 @@
     def pad_rows(value):
         return jnp.pad(value, [(0, 0)] * (value.ndim - 2) + [(0, -value.shape[-2] % 16), (0, 0)])
 
-    turned_cols = hidden_own + 3 * own
-    groups = turned_cols // chunk
+    up_groups = hidden_own // chunk
+    groups = up_groups + 1
     fine = own // (2 * ctx)
     turned = jnp.concatenate(
         [
             dot(normed_two_all, grad_hidden, ((0,), (0,))).astype(BF16),
-            dot(normed_all, grad_mixed, ((0,), (0,))).astype(BF16),
+            jnp.pad(
+                dot(normed_all, grad_mixed, ((0,), (0,))).astype(BF16),
+                ((0, 0), (0, chunk - 3 * own)),
+            ),
         ],
         axis=1,
     ).reshape(wsh, ctx, 2, fine, groups, chunk)
@@ -580,13 +586,11 @@
     back = summed[:, :, :at_down].reshape(ctx, 2, wsh, turned_rows, chunk)
     back = back[:, :, :, : groups * fine].reshape(ctx, 2, wsh, groups, fine, chunk)
 
-    def unturn(value, sections):
-        shaped = value.astype(F32).reshape(ctx, 2, wsh, sections, -1, fine, chunk)
-        return shaped.transpose(0, 1, 5, 3, 2, 4, 6).reshape(own, -1)
-
-    up_groups = hidden_own // chunk
-    grad_up_weight = unturn(back[:, :, :, :up_groups], 1)
-    grad_qkv_weight = unturn(back[:, :, :, up_groups:], 3)
+    up_back = back[:, :, :, :up_groups].astype(F32)
+    grad_up_weight = up_back.transpose(0, 1, 4, 2, 3, 5).reshape(own, -1)
+    qkv_back = back[:, :, :, up_groups, :, : 3 * own].astype(F32)
+    qkv_back = qkv_back.reshape(ctx, 2, wsh, fine, 3, own)
+    grad_qkv_weight = qkv_back.transpose(0, 1, 3, 4, 2, 5).reshape(own, -1)
     grad_down_weight = uncut(summed[:, :, at_down:at_dense], width)
     grad_dense_weight = uncut(summed[:, :, at_dense:at_vector], width)
     sums = summed[:, :, at_vector, :piece].reshape(-1).astype(F32)

time: 732 us -> 776 us (1.060)
  blocking collectives: 92.3 us -> 154 us
  waiting for transfers between devices: 224 us -> 191 us
  Pallas kernels: 189 us -> 210 us
    all_to_all x2 -> x1, waiting for transfers between devices: 64.4 us -> 0.01 us  [body(): lax.all_to_all(up_late.reshape(own, wsh, hidden_own), 'wsh', split_axis=1...]
    all_to_all x3 -> x4, blocking collectives: 80.9 us -> 121 us  [swap_ctx(): return lax.all_to_all(value, 'ctx', split_axis=0, concat_axis=0, tiled=True)]
    all_gather x4, waiting for transfers between devices: 24.3 us -> 55.5 us  [gather(): return lax.all_gather(value, 'wsh', axis=0, tiled=True)]
    all_gather x1, blocking collectives: 5.19 us -> 26.5 us  [gather(): return lax.all_gather(value, 'wsh', axis=0, tiled=True)]
    pallas_call x1, Pallas kernels: 141 us -> 162 us  [sum_over_ctx(): pl.pallas_call(functools.partial(sum_kernel, count, peers, turned), out_s...]
    reshape x10 -> x4, local copies, waits for them, and re-layouts: 31.9 us -> 20 us  [the longest x3 17.2 us: body(): grad_qkv_weight = qkv_back.transpose(0, 1, 3, 4, 2, 5).reshape(own, -1)]
    unnamed x74 -> x68, local copies, waits for them, and re-layouts: 24.3 us -> 24.9 us
  transfers between devices with their start and end apart: 12 -> 11, of which waited for: 9 -> 8; matrix products, arithmetic and copies ran while one was open for 12% -> 9% of each run, Pallas kernels for 0% -> 3%
where the time goes in v3:
time: 776 us; the launch traced here: 766 us
  Pallas kernels  210 us (27%)
  waiting for transfers between devices  191 us (25%)
  blocking collectives  154 us (20%)
  local copies, waits for them, and re-layouts  96 us (12%)
  matrix products  49.4 us (6%)
  other arithmetic  41.5 us (5%)
  between operations  14.8 us (2%)
  starting transfers between devices  9.79 us (1%)
    pallas_call x1, Pallas kernels, sum_over_ctx(): pl.pallas_call(functools.partial(sum_kernel, count, peers, turned), out_s...  162 us
    all_to_all x4, blocking collectives, swap_ctx(): return lax.all_to_all(value, 'ctx', split_axis=0, concat_axis=0, tiled=True)  121 us
    reduce_scatter x4, waiting for transfers between devices, scatter(): return lax.psum_scatter(value, 'wsh', scatter_dimension=0, tiled=True)  82.1 us
    all_gather x4, waiting for transfers between devices, gather(): return lax.all_gather(value, 'wsh', axis=0, tiled=True)  55.5 us
    pallas_call x2, Pallas kernels, call_local(): pl.pallas_call(kernel, out_shape=outs, in_specs=[smem] * 3 + [vmem] * (le...  48.2 us
    all_to_all x1, waiting for transfers between devices, body(): lax.all_to_all(qkv_weight.reshape(own, 3, wsh, own), 'wsh', split_axis=2,...  30.2 us
    dot_general x8, matrix products, dot(): return lax.dot_general(a, b, (dims, ((), ())), preferred_element_type=F32)  29.6 us
    all_gather x1, blocking collectives, gather(): return lax.all_gather(value, 'wsh', axis=0, tiled=True)  26.5 us
  transfers between devices with their start and end apart: 11, of which 8 were waited for; matrix products, arithmetic and copies ran while one was open for 9% of the time, Pallas kernels for 3%

profile of v3, /device:TPU:0, one launch (start us, length us, event | category | flops | bytes accessed | tf_op | source)
XLA Modules:
  0.0 766.3 jit_solution(14379835159625929960)
XLA Ops:
  13.9 6.2 all_gather.19
  27.5 4.4 all-to-all-start
  32.0 30.2 %all-to-all-done = bf16[256,3,4,256]{0,3,1,2:T(8,128)(2,1)} async-done(((bf16[256,3,4,256]{0,3,1,2:T(8,128)(2,1)}), bf16[256,3,4,256]{0,3,1,2:T(8,128)(2,1)}, u32[]{:S(2)}, u32[]{:S(2)}) %all-to-all-start) | async-done | bytes 1572896 | tf_op jit(solution)/shard_map/all_to_all | solution.py:403
  77.0 42.5 %all_to_all.50.packed_ref = bf16[8,768,128]{2,1,0:T(8,128)(2,1)} all-to-all(bf16[8,768,128]{2,1,0:T(8,128)(2,1)S(1)} %pad_maximum_fusion), channel_id=1, replica_groups=mesh['ctx'=8,'wsh'=4] {'ctx'}, dimensions={0} | all-to-all | bytes 3145728 | tf_op jit(solution)/shard_map/all_to_all | solution.py:395
  123.6 4.6 all-to-all-start.2
  128.4 26.5 %all-gather.1 = s32[4,1,2048]{2,1,0:T(1,128)S(1)} all-gather(s32[1,1,2048]{2,1,0:T(1,128)S(1)} %bitcast.253), channel_id=1, replica_groups=mesh['ctx'=8,'wsh'=4] {'wsh'}, dimensions={0}, use_global_device_ids=true | all-gather | bytes 40960 | tf_op jit(solution)/shard_map/all_gather | solution.py:389
  158.4 24.8 %shard_map.280 = (bf16[8,256,128]{2,1,0:T(8,128)(2,1)S(1)}, f32[128,2048]{1,0:T(8,128)S(1)}, f32[2,2048]{1,0:T(2,128)S(1)}) custom-call(s32[16]{0:T(128)S(1)} %select_reduce_fusion.order_ref, s32[8]{0:T(128)S(1)} %convert_reduce_fusion.4.count_ref, f32[2]{0:T(128)S(1)} %multiply_power_fusion.slope_ref, bf16[8,768,128]{2,1,0:T(8,128)(2,1)S(1)} %copy-done.3, ...), custom_call_target="tpu_custom_call" | custom-call | flops 2147483648 | bytes 6000000 | tf_op jit(solution)/shard_map/pallas_call | solution.py:222
  189.0 18.6 %all_to_all.51 = bf16[8,256,128]{2,1,0:T(8,128)(2,1)S(1)} all-to-all(bf16[8,256,128]{2,1,0:T(8,128)(2,1)} %copy-done.5), channel_id=1, replica_groups=mesh['ctx'=8,'wsh'=4] {'ctx'}, dimensions={0} | all-to-all | bytes 1048576 | tf_op jit(solution)/shard_map/all_to_all | solution.py:395
  212.1 29.6 %reduce-scatter.8.cloned.1.call-done = bf16[256,1024]{1,0:T(8,128)(2,1)} async-done(((bf16[1024,1024]{1,0:T(8,128)(2,1)}), bf16[256,1024]{1,0:T(8,128)(2,1)}) %reduce-scatter.8.cloned.1.call-update) | async-done | bytes 524304 | tf_op jit(solution)/shard_map/reduce_scatter | solution.py:392
  248.2 21.6 %all-gather.9.cloned.1.call-done = bf16[1024,1024]{1,0:T(8,128)(2,1)} async-done(((bf16[256,1024]{1,0:T(8,128)(2,1)}), bf16[1024,1024]{1,0:T(8,128)(2,1)}) %all-gather.9.cloned.1.call-update) | async-done | bytes 2097168 | tf_op jit(solution)/shard_map/all_gather | solution.py:389
  269.8 6.6 fusion.64
  276.4 17.6 %all-gather.13.cloned.1.call-done = bf16[1,1024,1024]{2,1,0:T(8,128)(2,1)} async-done(((bf16[1,256,1024]{2,1,0:T(8,128)(2,1)}), bf16[1,1024,1024]{2,1,0:T(8,128)(2,1)}) %all-gather.13.cloned.1.call-update) | async-done | bytes 2097168 | tf_op jit(solution)/shard_map/all_gather | solution.py:389
  294.0 7.5 fusion.62
  306.5 31.5 %reduce-scatter.10.cloned.1.call-done = bf16[256,1024]{1,0:T(8,128)(2,1)} async-done(((bf16[1024,1024]{1,0:T(8,128)(2,1)}), bf16[256,1024]{1,0:T(8,128)(2,1)}) %reduce-scatter.10.cloned.1.call-update) | async-done | bytes 524304 | tf_op jit(solution)/shard_map/reduce_scatter | solution.py:392
  343.4 6.3 convolution_convert_fusion.2
  349.7 16.3 %all-gather.11.cloned.1.call-done = bf16[1024,1024]{1,0:T(8,128)(2,1)} async-done(((bf16[256,1024]{1,0:T(8,128)(2,1)}), bf16[1024,1024]{1,0:T(8,128)(2,1)}) %all-gather.11.cloned.1.call-update) | async-done | bytes 2097168 | tf_op jit(solution)/shard_map/all_gather | solution.py:389
  370.5 20.2 %all_to_all.52.grad_ref = bf16[8,256,128]{2,1,0:T(8,128)(2,1)S(1)} all-to-all(bf16[8,256,128]{2,1,0:T(8,128)(2,1)S(1)} %bitcast.222), channel_id=1, replica_groups=mesh['ctx'=8,'wsh'=4] {'ctx'}, dimensions={0} | all-to-all | bytes 1048576 | tf_op jit(solution)/shard_map/all_to_all | solution.py:395
  392.0 23.4 %shard_map.281 = bf16[8,768,128]{2,1,0:T(8,128)(2,1)S(1)} custom-call(s32[16]{0:T(128)S(1)} %select_reduce_fusion.order_ref, s32[8]{0:T(128)S(1)} %convert_reduce_fusion.4.count_ref, f32[2]{0:T(128)S(1)} %multiply_power_fusion.slope_ref, bf16[8,768,128]{2,1,0:T(8,128)(2,1)S(1)} %copy-done.4, f32[1,2048]{1,0:T(1,128)S(1)} %get-tuple-element.66.query_pos_ref, ...), custom_call_target="tpu_custom_call" | custom-call | flops 5368709120 | bytes 6000000 | tf_op jit(solution)/shard_map/pallas_call | solution.py:222
  415.3 39.6 %all_to_all.53 = bf16[8,768,128]{2,1,0:T(8,128)(2,1)S(1)} all-to-all(bf16[8,768,128]{2,1,0:T(8,128)(2,1)S(1)} %shard_map.281), channel_id=1, replica_groups=mesh['ctx'=8,'wsh'=4] {'ctx'}, dimensions={0} | all-to-all | bytes 3145728 | tf_op jit(solution)/shard_map/all_to_all | solution.py:395
  463.3 5.1 convolution_convert_fusion
  468.4 4.4 fusion.17
  479.2 6.4 copy.135
  485.6 7.8 %reshape.229 = bf16[4,8,2,16,2,1024]{5,4,3,2,1,0:T(2,128)(2,1)} reshape(bf16[1024,2048]{1,0:T(8,128)(2,1)} %copy.135) | data formatting | bytes 8388608 | tf_op jit(solution)/shard_map/reshape | solution.py:555
  493.4 5.7 copy.136
  504.1 20.9 %reduce-scatter.12.cloned.1.call-done = bf16[256,1024]{1,0:T(8,128)(2,1)} async-done(((bf16[1024,1024]{1,0:T(8,128)(2,1)}), bf16[256,1024]{1,0:T(8,128)(2,1)}) %reduce-scatter.12.cloned.1.call-update) | async-done | bytes 524304 | tf_op jit(solution)/shard_map/reduce_scatter | solution.py:392
  527.7 22.1 %reduce-scatter.16.cloned.1.call-done = f32[256,4]{1,0:T(8,128)} async-done(((f32[1024,4]{1,0:T(8,128)}), f32[256,4]{1,0:T(8,128)}) %reduce-scatter.16.cloned.1.call-update) | async-done | bytes 4112
  551.7 6.2 fusion.2.part_ref
  558.0 161.8 %shard_map.282 = bf16[8,2,224,1024]{3,2,1,0:T(8,128)(2,1)S(1)} custom-call(bf16[8,2,224,1024]{3,2,1,0:T(8,128)(2,1)} %fusion.2.part_ref), custom_call_target="tpu_custom_call" | custom-call | flops 3670016 | bytes 300000000 | tf_op jit(solution)/shard_map/pallas_call | solution.py:349
  736.3 5.8 copy.150
  742.1 5.9 reshape.246
  748.0 6.1 copy.139
  754.2 5.1 reshape.238
  (178 shorter events, 110.1 us)
Async XLA Ops:
  7.2 286.8 %copy-start = (bf16[1024,1024]{1,0:T(8,128)(2,1)S(1)}, bf16[1024,1024]{1,0:T(8,128)(2,1)}, u32[]{:S(2)}) copy-start(bf16[1024,1024]{1,0:T(8,128)(2,1)} %param.31) | copy-start | bytes 6291460
  7.2 59.1 %all-gather.7.cloned.1.call-start = ((), (), s32[]{:S(2)}) async-start(), calls=%async_computation.11 | async-start | bytes 2621440 | tf_op jit(solution)/shard_map/all_gather | solution.py:389
  24.8 7.1 copy-start.23
  24.8 7.1 copy-start.24
  27.5 34.6 %all-to-all-start = ((bf16[256,3,4,256]{0,3,1,2:T(8,128)(2,1)}), bf16[256,3,4,256]{0,3,1,2:T(8,128)(2,1)}, u32[]{:S(2)}, u32[]{:S(2)}) async-start(bf16[256,3,4,256]{0,3,1,2:T(8,128)(2,1)} %copy.121), calls=%async_computation | async-start | bytes 3145728 | tf_op jit(solution)/shard_map/all_to_all | solution.py:403
  123.6 4.7 copy-start.21
  123.6 4.8 copy-start.19
  123.6 61.5 %all-to-all-start.2 = ((bf16[256,4,1024]{0,2,1:T(8,128)(2,1)}), bf16[256,4,1024]{0,2,1:T(8,128)(2,1)}, u32[]{:S(2)}, u32[]{:S(2)}) async-start(bf16[256,4,1024]{0,2,1:T(8,128)(2,1)} %bitcast.205), calls=%async_computation.2 | async-start | bytes 4194304 | tf_op jit(solution)/shard_map/all_to_all | solution.py:457
  128.2 113.6 %reduce-scatter.8.cloned.1.call-start = ((), (), s32[]{:S(2)}) async-start(), calls=%async_computation.12 | async-start | bytes 2621440 | tf_op jit(solution)/shard_map/reduce_scatter | solution.py:392
  157.0 1.4 copy-start.3
  212.0 36.2 %copy-start.20 = (bf16[1024]{0:T(1024)(128)(2,1)S(1)}, bf16[1024]{0:T(1024)(128)(2,1)}, u32[]{:S(2)}) copy-start(bf16[1024]{0:T(1024)(128)(2,1)} %param.30) | copy-start | bytes 6148
  212.1 57.8 %all-gather.9.cloned.1.call-start = ((), (), s32[]{:S(2)}) async-start(), calls=%async_computation.13 | async-start | bytes 2621440 | tf_op jit(solution)/shard_map/all_gather | solution.py:389
  247.1 46.9 %all-gather.13.cloned.1.call-start = ((), (), s32[]{:S(2)}) async-start(), calls=%async_computation.18 | async-start | bytes 2621440 | tf_op jit(solution)/shard_map/all_gather | solution.py:389
  247.7 90.4 %reduce-scatter.10.cloned.1.call-start = ((), (), s32[]{:S(2)}) async-start(), calls=%async_computation.14 | async-start | bytes 2621440 | tf_op jit(solution)/shard_map/reduce_scatter | solution.py:392
  294.0 8.8 %copy-start.14 = (bf16[4,256,1,1024]{3,1,0,2:T(8,128)(2,1)S(1)}, bf16[4,256,1,1024]{3,1,0,2:T(8,128)(2,1)}, u32[]{:S(2)}) copy-start(bf16[4,256,1,1024]{3,1,0,2:T(8,128)(2,1)} %copy.128) | copy-start | bytes 6291460
  306.5 59.6 %all-gather.11.cloned.1.call-start = ((), (), s32[]{:S(2)}) async-start(), calls=%async_computation.15 | async-start | bytes 2621440 | tf_op jit(solution)/shard_map/all_gather | solution.py:389
  343.3 158.0 %reduce-scatter.14.cloned.1.call-start = ((), (), s32[]{:S(2)}) async-start(), calls=%async_computation.17 | async-start | bytes 2621440 | tf_op jit(solution)/shard_map/reduce_scatter | solution.py:392
  349.7 41.0 %copy-start.4 = (bf16[8,768,128]{2,1,0:T(8,128)(2,1)S(1)}, bf16[8,768,128]{2,1,0:T(8,128)(2,1)}, u32[]{:S(2)}) copy-start(bf16[8,768,128]{2,1,0:T(8,128)(2,1)} %all_to_all.50.packed_ref) | copy-start | bytes 4718596
  455.1 3.0 copy-start.15
  461.2 63.8 %reduce-scatter.12.cloned.1.call-start = ((), (), s32[]{:S(2)}) async-start(), calls=%async_computation.16 | async-start | bytes 2621440 | tf_op jit(solution)/shard_map/reduce_scatter | solution.py:392
  462.0 87.8 %reduce-scatter.16.cloned.1.call-start = ((), (), s32[]{:S(2)}) async-start(), calls=%async_computation.19 | async-start | bytes 655360
  463.2 5.1 copy-start.18
  463.2 5.1 copy-start.25
  468.4 4.4 copy-start.13
  468.4 4.5 copy-start.11
  472.8 2.1 copy-start.22
  493.4 7.9 %copy-start.8 = (bf16[1,256,1024]{2,1,0:T(8,128)(2,1)S(1)}, bf16[1,256,1024]{2,1,0:T(8,128)(2,1)}, u32[]{:S(2)}) copy-start(bf16[1,256,1024]{2,1,0:T(8,128)(2,1)} %param.17) | copy-start | bytes 1572868
  499.1 25.9 %copy-start.9 = (bf16[256,1024]{1,0:T(8,128)(2,1)S(1)}, bf16[256,1024]{1,0:T(8,128)(2,1)}, u32[]{:S(2)}) copy-start(bf16[256,1024]{1,0:T(8,128)(2,1)} %reduce-scatter.8.cloned.1.call-done) | copy-start | bytes 1572868
  500.2 24.8 %copy-start.12 = (f32[256,1024]{1,0:T(8,128)S(1)}, f32[256,1024]{1,0:T(8,128)}, u32[]{:S(2)}) copy-start(f32[256,1024]{1,0:T(8,128)} %get-tuple-element.42) | copy-start | bytes 3145732
  719.8 3.0 copy-start.2
  728.7 2.2 slice-start.1
  748.0 11.2 %copy-start.1 = (bf16[1024,1024]{1,0:T(8,128)(2,1)S(1)}, bf16[1024,1024]{1,0:T(8,128)(2,1)}, u32[]{:S(2)}) copy-start(bf16[1024,1024]{1,0:T(8,128)(2,1)} %param.31) | copy-start | bytes 6291460
  (8 other events, 8.7 us)
Sparse Core Ops, SparseCore 0:
  22.4 34.5 all-gather.6
  212.2 29.5 reduce-scatter.7
  247.2 22.5 all-gather.8
  271.3 22.5 all-gather.12
  306.6 31.4 reduce-scatter.9
  343.5 22.5 all-gather.10
  461.4 29.4 reduce-scatter.13
  493.6 31.3 reduce-scatter.11
  528.1 21.6 reduce-scatter.15
